TPU v7x, 32 devices: a whole 2x2x4 slice. The times are simulated.
32 devices in a mesh: rep: 4 (over y, x), fsdp: 8 (over z, core).
Axes of the slice: x: 2, y: 2, z: 4, core: 2. Of those that a mesh axis runs over, the one named last changes fastest.
Arguments:
- states: bfloat16 [128, 32, 5120], P('fsdp'), may hold values from -6 to 6
- labels: bfloat16 [128, 8], P('fsdp'), may hold values from -4 to 4
- lengths: int32 [128], P('fsdp'), may hold values from 1 to 32
- segments: int32 [128, 32], P('fsdp'), may hold values from 0 to 7, never falling along the last dimension, each value on 1 to 8 neighbouring positions
- destinations: int32 [128, 1], P('fsdp'), may hold values from 0 to 7; in each aligned block of 16 rows (0 to 15, 16 to 31, ...) at most 2 rows name the same one
- gain: float32 [5120], replicated, may hold values from 0.1 to 1.9
- head_in: bfloat16 [5120, 5120], P('fsdp', 'rep'), may hold values from -0.078125 to 0.078125
- head_out: float32 [5120], P('rep'), may hold values from -0.078125 to 0.078125
Outputs:
- step_rewards: float32 [128, 8], P('fsdp')
- head_grad: float32 [5120, 5120], P('fsdp', 'rep')
Inputs may be any that keep to these rules, and one draw needn't show every extreme that they name: `destinations`: among the 16 rows of one generator device no trainer index is named by more than 2 rows, a bound that some block reaches. `segments`: step numbers never fall along a row; every step has 1 to 8 slots, one step of each row exactly 8.
All inputs are finite; a program needn't handle non-finite values.
Results may differ from a plain program's by a relative error of at most 0.0052.
Values may be sent and summed in bfloat16 or wider, within the bound.
No kernel may reach another device: no remote copies, remote signals or barrier semaphores. Data moves between devices by JAX's collectives and lax.ppermute only.
A program may use at most 128 MiB of HBM per device.

v0:
```python
import functools
import math

import jax
import jax.numpy as jnp
from jax import lax
from jax.experimental import pallas as pl
from jax.experimental.pallas import tpu as pltpu
from jax.sharding import PartitionSpec as P

CAP = 2
STEPS = 8
LOCAL = 384
VMEM_BYTES = 52 * 1024 * 1024


def silu_slope(pre_act):
    sigma = jax.nn.sigmoid(pre_act)
    return sigma * (1.0 + pre_act * (1.0 - sigma))


def normalize(tokens_flat, gain):
    wide = tokens_flat.astype(jnp.float32)
    meansq = jnp.mean(wide * wide, axis=1, keepdims=True)
    return (wide * lax.rsqrt(meansq + 1e-06) * gain[None, :]).astype(jnp.bfloat16)


def member_of(segments, lengths):
    positions = jnp.arange(segments.shape[1], dtype=jnp.int32)
    valid = (positions[None, :] < lengths[:, None]).astype(jnp.float32)
    step_ids = jnp.arange(STEPS, dtype=jnp.int32)
    return (segments[:, :, None] == step_ids[None, None, :]).astype(jnp.float32) * valid[:, :, None]


def rank_of(target):
    order = jnp.arange(target.shape[0], dtype=jnp.int32)
    earlier = (target[:, None] == target[None, :]) & (order[None, :] < order[:, None])
    return jnp.sum(earlier.astype(jnp.int32), axis=1)


def gathered_weights(states, labels, lengths, segments, destinations, gain, head_in, head_out):
    row_count, slot_span, feature_width = states.shape
    trainers = lax.axis_size("fsdp")
    slot_total = trainers * CAP
    normed = normalize(states.reshape(-1, feature_width), gain)
    member = member_of(segments, lengths)
    live = jnp.max(member, axis=1)

    def scored(weights):
        pre_act = jnp.dot(normed, weights, preferred_element_type=jnp.float32)
        partial = jnp.sum(jax.nn.silu(pre_act) * head_out[None, :], axis=1)
        return pre_act, lax.psum(partial, "rep").reshape(row_count, slot_span)

    pre_act, score = scored(lax.all_gather(head_in, "fsdp", axis=0, tiled=True))
    step_score = jnp.einsum("rs,rsk->rk", score, member, precision=lax.Precision.HIGHEST)
    step_error = live * (step_score - labels.astype(jnp.float32))
    token_error = jnp.einsum("rk,rsk->rs", step_error, member, precision=lax.Precision.HIGHEST).reshape(-1)
    pre_grad = (token_error[:, None] * head_out[None, :] * silu_slope(pre_act)).astype(jnp.bfloat16)
    rate = 0.5 / math.sqrt(row_count * trainers * slot_span)
    head_grad = lax.psum_scatter(
        lax.dot_general(normed, pre_grad, (((0,), (0,)), ((), ())), preferred_element_type=jnp.float32),
        "fsdp",
        scatter_dimension=0,
        tiled=True,
    )
    fresh = (head_in.astype(jnp.float32) - rate * head_grad).astype(jnp.bfloat16)
    _, fresh_score = scored(lax.all_gather(fresh, "fsdp", axis=0, tiled=True))
    reward = jnp.einsum("rs,rsk->rk", fresh_score, member, precision=lax.Precision.HIGHEST)
    target = destinations[:, 0]
    slot = target * CAP + rank_of(target)
    placing = (slot[None, :] == jnp.arange(slot_total, dtype=jnp.int32)[:, None]).astype(jnp.float32)
    placed = jnp.dot(placing, reward, precision=lax.Precision.HIGHEST)
    return lax.all_to_all(placed, "fsdp", split_axis=0, concat_axis=0, tiled=True), head_grad


X_MATE = [(r, r ^ 1) for r in range(4)]
Y_MATE = [(r, r ^ 2) for r in range(4)]
XY_MATE = [(r, r ^ 3) for r in range(4)]
CORE_MATE = [(f, f ^ 1) for f in range(8)]
Z1_MATE = [(f, f ^ 2) for f in range(8)]
Z2_MATE = [(f, f ^ 4) for f in range(8)]
Z3_MATE = [(f, f ^ 6) for f in range(8)]
INNER = [(f, f ^ 6) for f in (2, 3, 4, 5)]
OUTWARD = [(f, f ^ 2) for f in (2, 3, 4, 5)]


def sum_over_chips(values):
    values = (values + lax.ppermute(values, "rep", X_MATE)) + (
        lax.ppermute(values, "rep", Y_MATE) + lax.ppermute(values, "rep", XY_MATE)
    )
    return (values + lax.ppermute(values, "fsdp", Z1_MATE)) + (
        lax.ppermute(values, "fsdp", Z2_MATE) + lax.ppermute(values, "fsdp", Z3_MATE)
    )


def core_swap(values):
    return lax.ppermute(values, "fsdp", CORE_MATE)


def sum_in_turn(values):
    for axis, pairs in (("rep", X_MATE), ("rep", Y_MATE), ("fsdp", Z1_MATE), ("fsdp", Z2_MATE)):
        values = values + lax.ppermute(values, axis, pairs)
    return values


def gather_small(values):
    copies = jnp.broadcast_to(values[None], (8,) + values.shape)
    return lax.all_to_all(copies, "fsdp", split_axis=0, concat_axis=0, tiled=True)


def around(part, own, inner, weights=None, facts=None):
    half = part.shape[0] // 32 * 16
    together = lax.optimization_barrier

    def along(values, pairs):
        return lax.ppermute(values, "fsdp", pairs)

    def x_of(values):
        return lax.ppermute(values, "rep", X_MATE)

    def y_of(values):
        return lax.ppermute(values, "rep", Y_MATE)

    a, b_in = together((along(part, Z1_MATE), along(part, INNER)))
    own, a = together((own, a))
    second = (x_of(a), y_of(a), along(b_in, OUTWARD), along(a, INNER))
    if facts is not None:
        facts = gather_small(facts)
        second, facts = together((second, facts))
    ax, ay, b_out, c_in = together(second)
    b = jnp.where(inner, b_in, b_out)
    c_out = along(c_in, OUTWARD)
    a_low, a_high, bx, by = together((y_of(ax[:half]), x_of(ay[half:]), x_of(b), y_of(b)))
    c_out, bx = together((c_out, bx))
    if weights is not None:
        weights, c_out = together((weights, c_out))
        weights = lax.all_to_all(
            weights, "fsdp", 0, 0, axis_index_groups=[[0, 2, 4, 6], [1, 3, 5, 7]], tiled=True
        )
    c = jnp.where(inner, c_in, c_out)
    fourth = (y_of(bx[:half]), x_of(by[half:]), x_of(c), y_of(c))
    if weights is not None:
        fourth, weights = together((fourth, weights))
    b_low, b_high, cx, cy = together(fourth)
    c_low, c_high = y_of(cx[:half]), x_of(cy[half:])
    parts = [own, a, ax, ay, a_low, a_high, b, bx, by, b_low, b_high, c, cx, cy, c_low, c_high]
    return parts, weights, facts


def step_sums(pre, share, spots, bounds_ref, sums_ref, first):
    score = jnp.sum(pre * jax.nn.sigmoid(pre) * share, axis=0, keepdims=True)
    span = spots.shape[2]
    for at in range(2):
        chip = first + at
        here = spots[at]
        low = bounds_ref[chip, :, 0:1]
        high = bounds_ref[chip, :, 1:2]
        inside = (here >= low) & (here < high)
        sums = jnp.sum(jnp.where(inside, score[:, at * span : (at + 1) * span], 0.0), axis=1, keepdims=True)
        sums_ref[chip] = jnp.broadcast_to(sums, sums_ref.shape[1:])


def first_kernel(offsets_ref, *refs, sizes, blocks):
    count = len(sizes)
    parts = refs[:count]
    own_w, mate_w, share_ref, spots_ref, bounds_ref = refs[count : count + 5]
    pre_ref, sums_ref, kept_ref, given_ref, x_s, w_s, acc_s, in_sem, w_sem, out_sem = refs[count + 5 :]
    wide = own_w.shape[2]
    copies = []
    at = 0
    for index, size in enumerate(sizes):
        copies.append(pltpu.make_async_copy(parts[index], x_s.at[pl.ds(at, size)], in_sem.at[index]))
        at += size
    weight_copies = []
    for core, source in enumerate((own_w, mate_w)):
        for j in range(4):
            where = pl.ds(pl.multiple_of(offsets_ref[core * 4 + j], 128), wide)
            weight_copies.append(
                pltpu.make_async_copy(source.at[j], w_s.at[:, where], w_sem.at[core * 4 + j])
            )
    for copy in weight_copies + copies:
        copy.start()
    for copy in weight_copies:
        copy.wait()
    total = x_s.shape[0]
    tile = total // 2
    depth = x_s.shape[1] // blocks
    out_copies = []
    waited = 0
    at = 0
    for half in range(2):
        while at < (half + 1) * tile:
            copies[waited].wait()
            at += sizes[waited]
            waited += 1
        rows = pl.ds(half * tile, tile)
        for core, dest in enumerate((kept_ref, given_ref)):
            for j in range(4):
                where = pl.ds(pl.multiple_of(offsets_ref[core * 4 + j], 128), wide)
                out_copies.append(
                    pltpu.make_async_copy(
                        x_s.at[rows, where], dest.at[j, rows], out_sem.at[half * 8 + core * 4 + j]
                    )
                )
                out_copies[-1].start()
        acc_s[...] = jnp.zeros_like(acc_s)

        @pl.loop(0, blocks)
        def _(k):
            where = pl.ds(pl.multiple_of(k * depth, 128), depth)
            acc_s[...] += lax.dot_general(
                w_s[:, where], x_s[rows, where], (((1,), (1,)), ((), ())), preferred_element_type=jnp.float32
            )

        pre = acc_s[...]
        pre_ref[:, half * tile : (half + 1) * tile] = pre
        step_sums(pre, share_ref[...], spots_ref[half * 2 : half * 2 + 2], bounds_ref, sums_ref, half * 2)
    for copy in out_copies:
        copy.wait()


def first_scores(parts, own_w, mate_w, share, spots, bounds, offsets):
    sizes = tuple(part.shape[0] for part in parts)
    total = sum(sizes)
    width = parts[0].shape[1]
    units, wide = own_w.shape[1:]
    anywhere = pl.BlockSpec(memory_space=pl.ANY)
    vmem = pl.BlockSpec(memory_space=pltpu.VMEM)
    return pl.pallas_call(
        functools.partial(first_kernel, sizes=sizes, blocks=5),
        out_shape=(
            jax.ShapeDtypeStruct((units, total), jnp.float32),
            jax.ShapeDtypeStruct((4, bounds.shape[1], 128), jnp.float32),
            jax.ShapeDtypeStruct((4, total, wide), jnp.bfloat16),
            jax.ShapeDtypeStruct((4, total, wide), jnp.bfloat16),
        ),
        in_specs=[pl.BlockSpec(memory_space=pltpu.SMEM)] + [anywhere] * (len(parts) + 2) + [vmem] * 3,
        out_specs=(vmem, vmem, anywhere, anywhere),
        scratch_shapes=[
            pltpu.VMEM((total, width), jnp.bfloat16),
            pltpu.VMEM((units, width), jnp.bfloat16),
            pltpu.VMEM((units, total // 2), jnp.float32),
            pltpu.SemaphoreType.DMA((len(parts),)),
            pltpu.SemaphoreType.DMA((8,)),
            pltpu.SemaphoreType.DMA((16,)),
        ],
        compiler_params=pltpu.CompilerParams(vmem_limit_bytes=VMEM_BYTES),
        cost_estimate=pl.CostEstimate(
            flops=2 * units * width * total, bytes_accessed=4 * total * width, transcendentals=units * total
        ),
        name="first_scores",
    )(offsets, *parts, own_w, mate_w, share, spots, bounds)


def fresh_kernel(kept_ref, given_ref, own_w, mate_w, share_ref, spots_ref, bounds_ref, sums_ref, acc_s):
    half = pl.program_id(0)
    k = pl.program_id(1)
    contract = (((1,), (1,)), ((), ()))
    term = lax.dot_general(own_w[0], kept_ref[0], contract, preferred_element_type=jnp.float32)
    term = term + lax.dot_general(mate_w[0], given_ref[0], contract, preferred_element_type=jnp.float32)

    @pl.when(k == 0)
    def _():
        acc_s[...] = term

    @pl.when(k > 0)
    def _():
        acc_s[...] += term

    @pl.when(k == 3)
    def _():
        step_sums(acc_s[...], share_ref[...], spots_ref[...], bounds_ref, sums_ref, 0)


def fresh_scores(kept, given, own_w, mate_w, share, spots, bounds):
    total, wide = kept.shape[1:]
    units = own_w.shape[1]
    steps = bounds.shape[1]
    tile = total // 2
    tokens = pl.BlockSpec((1, tile, wide), lambda h, k: (k, h, 0))
    weights = pl.BlockSpec((1, units, wide), lambda h, k: (k, 0, 0))
    return pl.pallas_call(
        fresh_kernel,
        grid=(2, 4),
        out_shape=jax.ShapeDtypeStruct((4, steps, 128), jnp.float32),
        in_specs=[
            tokens,
            tokens,
            weights,
            weights,
            pl.BlockSpec((units, 1), lambda h, k: (0, 0)),
            pl.BlockSpec((2,) + spots.shape[1:], lambda h, k: (h, 0, 0)),
            pl.BlockSpec((2, steps, 2), lambda h, k: (h, 0, 0)),
        ],
        out_specs=pl.BlockSpec((2, steps, 128), lambda h, k: (h, 0, 0)),
        scratch_shapes=[pltpu.VMEM((units, tile), jnp.float32)],
        compiler_params=pltpu.CompilerParams(vmem_limit_bytes=VMEM_BYTES),
        cost_estimate=pl.CostEstimate(
            flops=4 * units * wide * 4 * total, bytes_accessed=16 * total * wide, transcendentals=units * total
        ),
        name="fresh_scores",
    )(kept, given, own_w, mate_w, share, spots, bounds)


def grad_kernel(rate, count, *refs):
    head_ref = refs[0]
    ins = refs[1 : 1 + 2 * count]
    grad_ref, fresh_ref = refs[1 + 2 * count :]
    grad = jnp.dot(ins[0][...], ins[1][0], preferred_element_type=jnp.float32)
    for at in range(2, 2 * count, 2):
        grad = grad + jnp.dot(ins[at][...], ins[at + 1][0], preferred_element_type=jnp.float32)
    grad_ref[0] = grad.astype(grad_ref.dtype)
    fresh_ref[0] = (head_ref[0].astype(jnp.float32) - rate * grad).astype(fresh_ref.dtype)


def grads_and_fresh(head, terms, rate):
    units, wide = head.shape[1:]
    block = pl.BlockSpec((1, units, wide), lambda j: (j, 0, 0))
    specs = [block]
    flat = [head]
    work = 0
    for pre_grad, tokens in terms:
        specs.append(pl.BlockSpec(pre_grad.shape, lambda j: (0, 0)))
        specs.append(pl.BlockSpec((1,) + tokens.shape[1:], lambda j: (j, 0, 0)))
        flat += [pre_grad, tokens]
        work += tokens.size
    return pl.pallas_call(
        functools.partial(grad_kernel, rate, len(terms)),
        grid=(4,),
        out_shape=(jax.ShapeDtypeStruct(head.shape, jnp.bfloat16),) * 2,
        in_specs=specs,
        out_specs=(block, block),
        compiler_params=pltpu.CompilerParams(vmem_limit_bytes=VMEM_BYTES),
        cost_estimate=pl.CostEstimate(flops=2 * units * work, bytes_accessed=2 * work, transcendentals=0),
        name="grads_and_fresh",
    )(*flat)


def spread_tokens(states, labels, lengths, segments, destinations, gain, head_in, head_out):
    row_count, slot_span, width = states.shape
    tokens_most = row_count * slot_span
    f = lax.axis_index("fsdp")
    r = lax.axis_index("rep")
    z = f // 2
    c = f % 2
    inner = (z == 1) | (z == 2)
    units = head_in.shape[1] // 4
    wide = head_in.shape[0]
    flat_states = states.reshape(-1, width)

    row_ids = jnp.arange(row_count)
    ends_row = jnp.sum(jnp.where(row_ids[:, None] >= row_ids[None, :], lengths[None, :], 0), axis=1)
    place = jnp.where(
        jnp.arange(slot_span)[None, :] < lengths[:, None],
        (ends_row - lengths)[:, None] + jnp.arange(slot_span)[None, :],
        -1,
    ).reshape(-1)

    def compacted(first, count):
        spots = first + jnp.arange(count, dtype=jnp.int32)
        picks = (place[None, :] == spots[:, None]).astype(jnp.bfloat16)
        tokens = jnp.dot(picks, flat_states, preferred_element_type=jnp.float32)
        return normalize(tokens.astype(jnp.bfloat16), gain)

    def gathered(first, count, weights=None, facts=None):
        quarter = count // 4
        mine = compacted(first + r * quarter, quarter)
        parts, weights, facts = around(mine, compacted(first, count), inner, weights, facts)
        plain = (first + jnp.arange(count))[None, :]
        moved = jnp.concatenate([first + (r ^ j) * quarter + jnp.arange(quarter) for j in range(4)])[None, :]
        spots = jnp.stack([plain, moved, moved, moved]).astype(jnp.float32)
        return parts, spots, weights, facts

    counts = jnp.sum(member_of(segments, lengths), axis=1)
    target = destinations[:, 0]
    slot_of = target * (8 * CAP) + f * CAP + rank_of(target)
    facts = jnp.concatenate(
        [counts.reshape(-1), labels.astype(jnp.float32).reshape(-1), slot_of.astype(jnp.float32)]
    )
    facts = jnp.pad(facts, (0, 384 - facts.shape[0]))
    head_t = jnp.transpose(head_in).reshape(4, units, wide)
    main_parts, main_spots, own_head, facts_all = gathered(0, LOCAL, head_t, facts)
    steps = row_count * STEPS
    counts_all = facts_all[:, :steps]
    labels_all = facts_all[:, steps : 2 * steps]
    slots_all = facts_all[:, 2 * steps : 2 * steps + row_count].reshape(-1)
    upto = jnp.arange(steps)[:, None] >= jnp.arange(steps)[None, :]
    ends_all = jnp.sum(jnp.where(upto[None], counts_all[:, None, :], 0.0), axis=2)
    lows_all = ends_all - counts_all
    overflow = jnp.max(ends_all[:, steps - 1]) > LOCAL

    sources = [z, z ^ 1, jnp.where(z < 2, 2, 1), jnp.where(z < 2, 3, 0)]
    takes = [jnp.arange(8) == source * 2 + c for source in sources]

    def of_chips(values):
        return jnp.stack([jnp.sum(jnp.where(take[:, None], values, 0.0), axis=0) for take in takes])

    bounds = jnp.stack([of_chips(lows_all), of_chips(ends_all)], axis=2)
    labels_here = of_chips(labels_all)
    live_here = jnp.minimum(of_chips(counts_all), 1.0)

    def of_lines(chip_sums):
        return sum(jnp.where(take[:, None], chip_sums[i][None, :], 0.0) for i, take in enumerate(takes))

    mate_head = core_swap(own_head)
    share = lax.dynamic_slice_in_dim(head_out, z * units, units)[:, None]
    rate = 0.5 / math.sqrt(row_count * 8 * slot_span)
    blocks_at = [(j * 2 + core) * wide for core in (c, 1 - c) for j in range(4)]
    offsets = jnp.stack(blocks_at).astype(jnp.int32)

    def scored(parts, spots):
        return first_scores(parts, own_head, mate_head, share, spots, bounds, offsets)

    def pre_grad_of(pre, spots, step_error):
        errors = []
        for i in range(4):
            inside = (spots[i] >= bounds[i, :, 0:1]) & (spots[i] < bounds[i, :, 1:2])
            errors.append(jnp.sum(jnp.where(inside, step_error[i][:, None], 0.0), axis=0))
        return (jnp.concatenate(errors)[None, :] * share * silu_slope(pre)).astype(jnp.bfloat16)

    def rest_of(batches):
        chip_sums = sum(sums[:, :, 0] for _, (_, sums, _, _) in batches)
        step_score = of_chips(sum_over_chips(of_lines(chip_sums)))
        step_error = live_here * (step_score - labels_here)
        terms = []
        for spots, (pre, _, kept, given) in batches:
            pre_grad = pre_grad_of(pre, spots, step_error)
            terms += [(pre_grad, kept), (core_swap(pre_grad), core_swap(given))]
        grads, own_fresh = grads_and_fresh(own_head, terms, rate)
        returned = lax.all_to_all(
            grads, "fsdp", 0, 0, axis_index_groups=[[0, 2, 4, 6], [1, 3, 5, 7]], tiled=True
        )
        mate_fresh = core_swap(own_fresh)
        fresh_sums = sum(
            fresh_scores(kept, given, own_fresh, mate_fresh, share, spots, bounds)[:, :, 0]
            for spots, (_, _, kept, given) in batches
        )
        lines = of_lines(fresh_sums)
        lines = lines + core_swap(lines)
        reward = sum_in_turn(lines).reshape(8 * row_count, STEPS)
        wanted = f * (8 * CAP) + jnp.arange(8 * CAP, dtype=jnp.int32)
        hits = slots_all[None, :] == wanted[:, None].astype(jnp.float32)
        step_rewards = jnp.sum(jnp.where(hits[:, :, None], reward[None], 0.0), axis=1)
        head_grad = jnp.transpose(returned.reshape(4 * units, wide)).astype(jnp.float32)
        return step_rewards, head_grad

    main_batch = (main_spots, scored(main_parts, main_spots))
    if LOCAL == tokens_most:
        return rest_of([main_batch])

    def with_more():
        more_parts, more_spots, _, _ = gathered(LOCAL, tokens_most - LOCAL)
        return rest_of([main_batch, (more_spots, scored(more_parts, more_spots))])

    return lax.cond(overflow, with_more, lambda: rest_of([main_batch]))


def solution(mesh):
    in_specs = (
        P("fsdp", None, None),
        P("fsdp", None),
        P("fsdp"),
        P("fsdp", None),
        P("fsdp", None),
        P(),
        P("fsdp", "rep"),
        P("rep"),
    )
    out_specs = (P("fsdp", None), P("fsdp", "rep"))

    def local(states, *rest):
        if lax.axis_size("rep") == 4 and lax.axis_size("fsdp") == 8:
            return spread_tokens(states, *rest)
        return gathered_weights(states, *rest)

    return jax.shard_map(local, mesh=mesh, in_specs=in_specs, out_specs=out_specs, check_vma=False)
```

profile of v0, /device:TPU:0, one launch (start us, length us, event | category | flops | bytes accessed | tf_op | source)
XLA Modules:
  0.0 265.1 jit_solution(16543181696802834132)
XLA Ops:
  3.4 3.8 %multiply_reduce_fusion.2 = (f32[96]{0:T(128)S(1)}, f32[96,5120]{1,0:T(8,128)S(1)}) fusion(bf16[512,5120]{1,0:T(8,128)(2,1)} %bitcast.130, s32[512]{0:T(512)S(1)} %select_n.236, s32[96]{0:T(128)S(1)} %get-tuple-element.562), kind=kOutput, calls=%fused_computation.138 | convolution fusion | flops 505331616 | bytes 7211776 | tf_op jit(solution)/shard_map/dot_general | solution.py:362
  7.5 3.1 %collective-permute-start.47 = (bf16[96,5120]{1,0:T(8,128)(2,1)S(1)}, bf16[96,5120]{1,0:T(8,128)(2,1)S(1)}, u32[]{:S(2)}, u32[]{:S(2)}) collective-permute-start(bf16[96,5120]{1,0:T(8,128)(2,1)S(1)} %multiply_convert_fusion.5), channel_id=1, source_target_pairs={{0,2},{1,3},{2,0},{3,1},{4,6},{5,7},{6,4},{7,5},{8,10},{9,11},{10,... | collective-permute-start | bytes 2949128 | tf_op jit(solution)/shard_map/ppermute | solution.py:116
  12.2 2.4 fusion.12
  14.7 3.2 %fusion.14.refs_0_ = bf16[384,5120]{1,0:T(8,128)(2,1)} fusion(bf16[384,5120]{1,0:T(8,128)(2,1)S(1)} %get-tuple-element.556, f32[5120]{0:T(1024)S(1)} %copy-done.20, f32[384]{0:T(512)S(1)} %add_rsqrt_fusion.2), kind=kLoop, calls=%fused_computation.133 | loop fusion | flops 7864320 | bytes 7886336 | tf_op jit(solution)/shard_map/convert_element_type | solution.py:25
  17.8 14.5 %collective-permute-done.47.refs_1_ = bf16[96,5120]{1,0:T(8,128)(2,1)S(1)} collective-permute-done((bf16[96,5120]{1,0:T(8,128)(2,1)S(1)}, bf16[96,5120]{1,0:T(8,128)(2,1)S(1)}, u32[]{:S(2)}, u32[]{:S(2)}) %collective-permute-start.47) | collective-permute-done | bytes 983072 | tf_op jit(solution)/shard_map/ppermute | solution.py:116
  39.7 9.0 %all-to-all-start.2 = ((f32[8,1,384]{2,1,0:T(1,128)}), f32[8,1,384]{2,1,0:T(1,128)S(1)}, u32[]{:S(2)}, u32[]{:S(2)}) async-start(f32[8,1,384]{2,1,0:T(1,128)} %broadcast_in_dim.585), calls=%async_computation.2 | async-start | bytes 24576 | tf_op jit(solution)/shard_map/all_to_all | solution.py:108
  48.6 16.7 %all-to-all-done.2 = f32[8,1,384]{2,1,0:T(1,128)S(1)} async-done(((f32[8,1,384]{2,1,0:T(1,128)}), f32[8,1,384]{2,1,0:T(1,128)S(1)}, u32[]{:S(2)}, u32[]{:S(2)}) %all-to-all-start.2) | async-done | bytes 12320 | tf_op jit(solution)/shard_map/all_to_all | solution.py:108
  73.7 3.5 %copy.51 = bf16[1280,640]{1,0:T(8,128)(2,1)} copy(bf16[1280,640]{0,1:T(8,128)(2,1)} %bitcast.136) | data formatting | bytes 3276800 | tf_op jit(solution)/shard_map/transpose | solution.py:381
  77.2 24.7 %collective-permute-done.53.refs_4_ = bf16[48,5120]{1,0:T(8,128)(2,1)S(1)} collective-permute-done((bf16[48,5120]{1,0:T(8,128)(2,1)}, bf16[48,5120]{1,0:T(8,128)(2,1)S(1)}, u32[]{:S(2)}, u32[]{:S(2)}) %collective-permute-start.53) | collective-permute-done | bytes 491552 | tf_op jit(solution)/shard_map/ppermute | solution.py:122
  102.0 3.6 %all-to-all-start.3 = ((bf16[4,320,640]{2,1,0:T(8,128)(2,1)}), bf16[4,320,640]{2,1,0:T(8,128)(2,1)S(1)}, u32[]{:S(2)}, u32[]{:S(2)}) async-start(bf16[4,320,640]{2,1,0:T(8,128)(2,1)} %bitcast.135), calls=%async_computation.3 | async-start | bytes 3276800 | tf_op jit(solution)/shard_map/all_to_all | solution.py:137
  113.3 28.1 %collective-permute-done.58.refs_9_ = bf16[48,5120]{1,0:T(8,128)(2,1)S(1)} collective-permute-done((bf16[48,5120]{1,0:T(8,128)(2,1)S(1)}, bf16[48,5120]{1,0:T(8,128)(2,1)S(1)}, u32[]{:S(2)}, u32[]{:S(2)}) %collective-permute-start.58) | collective-permute-done | bytes 491552 | tf_op jit(solution)/shard_map/ppermute | solution.py:122
  158.4 3.5 %collective-permute-done.62.refs_14_ = bf16[48,5120]{1,0:T(8,128)(2,1)} collective-permute-done((bf16[48,5120]{1,0:T(8,128)(2,1)}, bf16[48,5120]{1,0:T(8,128)(2,1)}, u32[]{:S(2)}, u32[]{:S(2)}) %collective-permute-start.62) | collective-permute-done | bytes 491552 | tf_op jit(solution)/shard_map/ppermute | solution.py:122
  164.0 15.2 %first_scores.3 = (f32[320,1536]{1,0:T(8,128)}, f32[4,128,128]{2,1,0:T(8,128)}, bf16[4,1536,640]{2,1,0:T(8,128)(2,1)}, bf16[4,1536,640]{2,1,0:T(8,128)(2,1)}) custom-call(s32[8]{0:T(128)} %stack.160.offsets_ref, bf16[384,5120]{1,0:T(8,128)(2,1)} %fusion.14.refs_0_, bf16[96,5120]{1,0:T(8,128)(2,1)} %copy-done.12, bf16[96,5120]{1,0:T(8,128)(2,1)} %copy-done.5, ...), custom_call_target="tpu_custom_call" | custom-call | flops 5033164800 | bytes 31457280 | tf_op jit(solution)/shard_map/first_scores/pallas_call | solution.py:229
  179.3 85.8 %conditional.3 = (f32[16,8]{0,1:T(8,128)}, f32[640,1280]{1,0:T(8,128)}) conditional(s32[]{:T(128)} %convert_element_type.108, (f32[8,16]{1,0:T(8,128)}, s32[]{:T(128)}, pred[8]{0:T(512)(128)(4,1)}, f32[4,1,384]{2,1,0:T(1,128)S(1)}, f32[4,128,1]{1,0,2:T(4,128)}, /*index=5*/f32[4,128,1]{1,0,2:T(4,128)}, f32[4,128,128]{2,1,0:T(8,128)}, ...), branch_computations={%region_23.33_spmd, %region_33.49_spmd} | conditional | flops 15953286144 | bytes 221575936
  186.4 2.4 collective-permute-done.2
  194.7 3.2 %collective-permute-done.5 = f32[8,128]{1,0:T(8,128)S(1)} collective-permute-done((f32[8,128]{1,0:T(8,128)S(1)}, f32[8,128]{1,0:T(8,128)S(1)}, u32[]{:S(2)}, u32[]{:S(2)}) %collective-permute-start.5) | collective-permute-done | bytes 4128 | tf_op jit(solution)/shard_map/cond/branch_0_fun/ppermute | solution.py:92
  202.2 2.6 collective-permute-done.6.refs_3_
  204.8 10.8 %grads_and_fresh.2 = (bf16[4,320,640]{2,1,0:T(8,128)(2,1)}, bf16[4,320,640]{2,1,0:T(8,128)(2,1)}) custom-call(bf16[4,320,640]{2,1,0:T(8,128)(2,1)S(1)} %get-tuple-element.109.refs_0_, bf16[320,1536]{1,0:T(8,128)(2,1)S(1)} %multiply_convert_fusion.refs_1_, bf16[4,1536,640]{2,1,0:T(8,128)(2,1)} %get-tuple-element.107.refs_2_.kept_ref, ...), custom_call_target="tpu_custom_call" | custom-call | flops 5033164800 | bytes 15728640 | tf_op jit(solution)/shard_map/cond/branch_0_fun/grads_and_fresh/pallas_call | solution.py:327
  215.8 4.4 %all-to-all-start = ((bf16[4,320,640]{2,1,0:T(8,128)(2,1)}), bf16[4,320,640]{2,1,0:T(8,128)(2,1)}, u32[]{:S(2)}, u32[]{:S(2)}) async-start(bf16[4,320,640]{2,1,0:T(8,128)(2,1)} %get-tuple-element.123), calls=%async_computation | async-start | bytes 3276800 | tf_op jit(solution)/shard_map/cond/branch_0_fun/all_to_all | solution.py:430
  221.7 13.1 %fresh_scores.3 = f32[4,128,128]{2,1,0:T(8,128)S(1)} custom-call(bf16[4,1536,640]{2,1,0:T(8,128)(2,1)} %get-tuple-element.107.refs_2_.kept_ref, bf16[4,1536,640]{2,1,0:T(8,128)(2,1)} %get-tuple-element.108.given_ref, bf16[4,320,640]{2,1,0:T(8,128)(2,1)} %get-tuple-element.121.own_w, bf16[4,320,640]{2,1,0:T(8,128)(2,1)} %copy-done.8, ...), custom_call_target="tpu_custom_call" | custom-call | flops 5033164800 | bytes 15728640 | tf_op jit(solution)/shard_map/cond/branch_0_fun/fresh_scores/pallas_call | solution.py:282
  240.6 3.1 %collective-permute-done.11 = f32[8,128]{1,0:T(8,128)S(1)} collective-permute-done((f32[8,128]{1,0:T(8,128)S(1)}, f32[8,128]{1,0:T(8,128)S(1)}, u32[]{:S(2)}, u32[]{:S(2)}) %collective-permute-start.11) | collective-permute-done | bytes 4128 | tf_op jit(solution)/shard_map/cond/branch_0_fun/ppermute | solution.py:102
  247.6 4.5 %collective-permute-start.13 = (f32[8,128]{1,0:T(8,128)S(1)}, f32[8,128]{1,0:T(8,128)S(1)}, u32[]{:S(2)}, u32[]{:S(2)}) collective-permute-start(f32[8,128]{1,0:T(8,128)S(1)} %add.279), channel_id=1, source_target_pairs={{0,4},{1,5},{2,6},{3,7},{4,0},{5,1},{6,2},{7,3},{8,12},{9,13},{10,... | collective-permute-start | bytes 12296 | tf_op jit(solution)/shard_map/cond/branch_0_fun/ppermute | solution.py:102
  252.2 7.3 %collective-permute-done.13 = f32[8,128]{1,0:T(8,128)S(1)} collective-permute-done((f32[8,128]{1,0:T(8,128)S(1)}, f32[8,128]{1,0:T(8,128)S(1)}, u32[]{:S(2)}, u32[]{:S(2)}) %collective-permute-start.13) | collective-permute-done | bytes 4128 | tf_op jit(solution)/shard_map/cond/branch_0_fun/ppermute | solution.py:102
  262.1 3.0 %copy.67 = f32[640,1280]{1,0:T(8,128)} copy(f32[640,1280]{0,1:T(8,128)S(1)} %convert_bitcast_fusion) | data formatting | bytes 6553600 | tf_op jit(solution)/shard_map/conditional.1
  (198 shorter events, 77.6 us)
Async XLA Ops:
  7.5 24.8 %collective-permute-start.47 = (bf16[96,5120]{1,0:T(8,128)(2,1)S(1)}, bf16[96,5120]{1,0:T(8,128)(2,1)S(1)}, u32[]{:S(2)}, u32[]{:S(2)}) collective-permute-start(bf16[96,5120]{1,0:T(8,128)(2,1)S(1)} %multiply_convert_fusion.5), channel_id=1, source_target_pairs={{0,2},{1,3},{2,0},{3,1},{4,6},{5,7},{6,4},{7,5},{8,10},{9,11},{10,... | collective-permute-start | bytes 2949128 | tf_op jit(solution)/shard_map/ppermute | solution.py:116
  10.6 21.8 %collective-permute-start.48 = (bf16[96,5120]{1,0:T(8,128)(2,1)S(1)}, bf16[96,5120]{1,0:T(8,128)(2,1)}, u32[]{:S(2)}, u32[]{:S(2)}) collective-permute-start(bf16[96,5120]{1,0:T(8,128)(2,1)S(1)} %multiply_convert_fusion.5), channel_id=1, source_target_pairs={{2,4},{3,5},{4,2},{5,3},{10,12},{11,13},{12,10},{13,11},{18,20},{1... | collective-permute-start | bytes 2949128 | tf_op jit(solution)/shard_map/ppermute | solution.py:116
  32.3 33.0 %collective-permute-start.49 = (bf16[96,5120]{1,0:T(8,128)(2,1)S(1)}, bf16[96,5120]{1,0:T(8,128)(2,1)S(1)}, u32[]{:S(2)}, u32[]{:S(2)}) collective-permute-start(bf16[96,5120]{1,0:T(8,128)(2,1)S(1)} %collective-permute-done.47.refs_1_), channel_id=1, source_target_pairs={{0,8},{8,0},{16,24},{24,16},{1,9},{9,1},{17,25},{25,17},{2,10},{10... | collective-permute-start | bytes 2949128 | tf_op jit(solution)/shard_map/ppermute | solution.py:119
  34.0 31.4 %collective-permute-start.50 = (bf16[96,5120]{1,0:T(8,128)(2,1)S(1)}, bf16[96,5120]{1,0:T(8,128)(2,1)S(1)}, u32[]{:S(2)}, u32[]{:S(2)}) collective-permute-start(bf16[96,5120]{1,0:T(8,128)(2,1)S(1)} %collective-permute-done.47.refs_1_), channel_id=1, source_target_pairs={{0,16},{8,24},{16,0},{24,8},{1,17},{9,25},{17,1},{25,9},{2,18},{10... | collective-permute-start | bytes 2949128 | tf_op jit(solution)/shard_map/ppermute | solution.py:122
  35.5 29.9 %collective-permute-start.52 = (bf16[96,5120]{1,0:T(8,128)(2,1)S(1)}, bf16[96,5120]{1,0:T(8,128)(2,1)}, u32[]{:S(2)}, u32[]{:S(2)}) collective-permute-start(bf16[96,5120]{1,0:T(8,128)(2,1)S(1)} %collective-permute-done.47.refs_1_), channel_id=1, source_target_pairs={{2,4},{3,5},{4,2},{5,3},{10,12},{11,13},{12,10},{13,11},{18,20},{1... | collective-permute-start | bytes 2949128 | tf_op jit(solution)/shard_map/ppermute | solution.py:116
  37.1 28.3 %collective-permute-start.51 = (bf16[96,5120]{1,0:T(8,128)(2,1)}, bf16[96,5120]{1,0:T(8,128)(2,1)}, u32[]{:S(2)}, u32[]{:S(2)}) collective-permute-start(bf16[96,5120]{1,0:T(8,128)(2,1)} %collective-permute-done.48), channel_id=1, source_target_pairs={{2,0},{3,1},{4,6},{5,7},{10,8},{11,9},{12,14},{13,15},{18,16},{19,... | collective-permute-start | bytes 2949128 | tf_op jit(solution)/shard_map/ppermute | solution.py:116
  39.7 25.6 %all-to-all-start.2 = ((f32[8,1,384]{2,1,0:T(1,128)}), f32[8,1,384]{2,1,0:T(1,128)S(1)}, u32[]{:S(2)}, u32[]{:S(2)}) async-start(f32[8,1,384]{2,1,0:T(1,128)} %broadcast_in_dim.585), calls=%async_computation.2 | async-start | bytes 24576 | tf_op jit(solution)/shard_map/all_to_all | solution.py:108
  67.4 34.6 %collective-permute-start.55 = (bf16[96,5120]{1,0:T(8,128)(2,1)S(1)}, bf16[96,5120]{1,0:T(8,128)(2,1)}, u32[]{:S(2)}, u32[]{:S(2)}) collective-permute-start(bf16[96,5120]{1,0:T(8,128)(2,1)S(1)} %broadcast_select_fusion.3.refs_6_), channel_id=1, source_target_pairs={{0,8},{8,0},{16,24},{24,16},{1,9},{9,1},{17,25},{25,17},{2,10},{10... | collective-permute-start | bytes 2949128 | tf_op jit(solution)/shard_map/ppermute | solution.py:119
  68.0 34.0 %collective-permute-start.56 = (bf16[96,5120]{1,0:T(8,128)(2,1)S(1)}, bf16[96,5120]{1,0:T(8,128)(2,1)}, u32[]{:S(2)}, u32[]{:S(2)}) collective-permute-start(bf16[96,5120]{1,0:T(8,128)(2,1)S(1)} %broadcast_select_fusion.3.refs_6_), channel_id=1, source_target_pairs={{0,16},{8,24},{16,0},{24,8},{1,17},{9,25},{17,1},{25,9},{2,18},{10... | collective-permute-start | bytes 2949128 | tf_op jit(solution)/shard_map/ppermute | solution.py:122
  68.5 33.5 %collective-permute-start.57 = (bf16[96,5120]{1,0:T(8,128)(2,1)}, bf16[96,5120]{1,0:T(8,128)(2,1)}, u32[]{:S(2)}, u32[]{:S(2)}) collective-permute-start(bf16[96,5120]{1,0:T(8,128)(2,1)} %collective-permute-done.52), channel_id=1, source_target_pairs={{2,0},{3,1},{4,6},{5,7},{10,8},{11,9},{12,14},{13,15},{18,16},{19,... | collective-permute-start | bytes 2949128 | tf_op jit(solution)/shard_map/ppermute | solution.py:116
  70.6 31.4 %collective-permute-start.53 = (bf16[48,5120]{1,0:T(8,128)(2,1)}, bf16[48,5120]{1,0:T(8,128)(2,1)S(1)}, u32[]{:S(2)}, u32[]{:S(2)}) collective-permute-start(bf16[48,5120]{1,0:T(8,128)(2,1)} %slice.269), channel_id=1, source_target_pairs={{0,16},{8,24},{16,0},{24,8},{1,17},{9,25},{17,1},{25,9},{2,18},{10... | collective-permute-start | bytes 1474568 | tf_op jit(solution)/shard_map/ppermute | solution.py:122
  72.2 29.8 %collective-permute-start.54 = (bf16[48,5120]{1,0:T(8,128)(2,1)S(1)}, bf16[48,5120]{1,0:T(8,128)(2,1)S(1)}, u32[]{:S(2)}, u32[]{:S(2)}) collective-permute-start(bf16[48,5120]{1,0:T(8,128)(2,1)S(1)} %slice.270), channel_id=1, source_target_pairs={{0,8},{8,0},{16,24},{24,16},{1,9},{9,1},{17,25},{25,17},{2,10},{10... | collective-permute-start | bytes 1474568 | tf_op jit(solution)/shard_map/ppermute | solution.py:119
  102.0 41.4 %all-to-all-start.3 = ((bf16[4,320,640]{2,1,0:T(8,128)(2,1)}), bf16[4,320,640]{2,1,0:T(8,128)(2,1)S(1)}, u32[]{:S(2)}, u32[]{:S(2)}) async-start(bf16[4,320,640]{2,1,0:T(8,128)(2,1)} %bitcast.135), calls=%async_computation.3 | async-start | bytes 3276800 | tf_op jit(solution)/shard_map/all_to_all | solution.py:137
  106.9 34.4 %collective-permute-start.60 = (bf16[96,5120]{1,0:T(8,128)(2,1)S(1)}, bf16[96,5120]{1,0:T(8,128)(2,1)S(1)}, u32[]{:S(2)}, u32[]{:S(2)}) collective-permute-start(bf16[96,5120]{1,0:T(8,128)(2,1)S(1)} %broadcast_select_fusion.2.refs_11_), channel_id=1, source_target_pairs={{0,8},{8,0},{16,24},{24,16},{1,9},{9,1},{17,25},{25,17},{2,10},{10... | collective-permute-start | bytes 2949128 | tf_op jit(solution)/shard_map/ppermute | solution.py:119
  108.5 34.6 %collective-permute-start.61 = (bf16[96,5120]{1,0:T(8,128)(2,1)S(1)}, bf16[96,5120]{1,0:T(8,128)(2,1)}, u32[]{:S(2)}, u32[]{:S(2)}) collective-permute-start(bf16[96,5120]{1,0:T(8,128)(2,1)S(1)} %broadcast_select_fusion.2.refs_11_), channel_id=1, source_target_pairs={{0,16},{8,24},{16,0},{24,8},{1,17},{9,25},{17,1},{25,9},{2,18},{10... | collective-permute-start | bytes 2949128 | tf_op jit(solution)/shard_map/ppermute | solution.py:122
  110.1 31.3 %collective-permute-start.58 = (bf16[48,5120]{1,0:T(8,128)(2,1)S(1)}, bf16[48,5120]{1,0:T(8,128)(2,1)S(1)}, u32[]{:S(2)}, u32[]{:S(2)}) collective-permute-start(bf16[48,5120]{1,0:T(8,128)(2,1)S(1)} %slice.271), channel_id=1, source_target_pairs={{0,16},{8,24},{16,0},{24,8},{1,17},{9,25},{17,1},{25,9},{2,18},{10... | collective-permute-start | bytes 1474568 | tf_op jit(solution)/shard_map/ppermute | solution.py:122
  112.7 28.7 %collective-permute-start.59 = (bf16[48,5120]{1,0:T(8,128)(2,1)S(1)}, bf16[48,5120]{1,0:T(8,128)(2,1)S(1)}, u32[]{:S(2)}, u32[]{:S(2)}) collective-permute-start(bf16[48,5120]{1,0:T(8,128)(2,1)S(1)} %slice.272), channel_id=1, source_target_pairs={{0,8},{8,0},{16,24},{24,16},{1,9},{9,1},{17,25},{25,17},{2,10},{10... | collective-permute-start | bytes 1474568 | tf_op jit(solution)/shard_map/ppermute | solution.py:119
  143.4 20.6 %collective-permute-start.64 = (bf16[4,320,640]{2,1,0:T(8,128)(2,1)S(1)}, bf16[4,320,640]{2,1,0:T(8,128)(2,1)}, u32[]{:S(2)}, u32[]{:S(2)}) collective-permute-start(bf16[4,320,640]{2,1,0:T(8,128)(2,1)S(1)} %all-to-all-done.3.refs_16_), channel_id=1, source_target_pairs={{0,1},{1,0},{2,3},{3,2},{4,5},{5,4},{6,7},{7,6},{8,9},{9,8},{10,11... | collective-permute-start | bytes 4915208 | tf_op jit(solution)/shard_map/ppermute | solution.py:97
  147.9 13.9 %collective-permute-start.62 = (bf16[48,5120]{1,0:T(8,128)(2,1)}, bf16[48,5120]{1,0:T(8,128)(2,1)}, u32[]{:S(2)}, u32[]{:S(2)}) collective-permute-start(bf16[48,5120]{1,0:T(8,128)(2,1)} %slice.273), channel_id=1, source_target_pairs={{0,16},{8,24},{16,0},{24,8},{1,17},{9,25},{17,1},{25,9},{2,18},{10... | collective-permute-start | bytes 1474568 | tf_op jit(solution)/shard_map/ppermute | solution.py:122
  150.3 13.7 %collective-permute-start.63 = (bf16[48,5120]{1,0:T(8,128)(2,1)}, bf16[48,5120]{1,0:T(8,128)(2,1)}, u32[]{:S(2)}, u32[]{:S(2)}) collective-permute-start(bf16[48,5120]{1,0:T(8,128)(2,1)} %slice.274), channel_id=1, source_target_pairs={{0,8},{8,0},{16,24},{24,16},{1,9},{9,1},{17,25},{25,17},{2,10},{10... | collective-permute-start | bytes 1474568 | tf_op jit(solution)/shard_map/ppermute | solution.py:119
  179.4 25.4 %collective-permute-start.7 = (bf16[4,1536,640]{2,1,0:T(8,128)(2,1)}, bf16[4,1536,640]{2,1,0:T(8,128)(2,1)}, u32[]{:S(2)}, u32[]{:S(2)}) collective-permute-start(bf16[4,1536,640]{2,1,0:T(8,128)(2,1)} %get-tuple-element.108.given_ref), channel_id=1, source_target_pairs={{0,1},{1,0},{2,3},{3,2},{4,5},{5,4},{6,7},{7,6},{8,9},{9,8},{10,11... | collective-permute-start | bytes 23592968 | tf_op jit(solution)/shard_map/cond/branch_0_fun/ppermute | solution.py:97
  192.5 5.4 %collective-permute-start.5 = (f32[8,128]{1,0:T(8,128)S(1)}, f32[8,128]{1,0:T(8,128)S(1)}, u32[]{:S(2)}, u32[]{:S(2)}) collective-permute-start(f32[8,128]{1,0:T(8,128)S(1)} %add_add_fusion.1), channel_id=1, source_target_pairs={{0,6},{1,7},{2,4},{3,5},{4,2},{5,3},{6,0},{7,1},{8,14},{9,15},{10,... | collective-permute-start | bytes 12296 | tf_op jit(solution)/shard_map/cond/branch_0_fun/ppermute | solution.py:92
  215.8 44.7 %all-to-all-start = ((bf16[4,320,640]{2,1,0:T(8,128)(2,1)}), bf16[4,320,640]{2,1,0:T(8,128)(2,1)}, u32[]{:S(2)}, u32[]{:S(2)}) async-start(bf16[4,320,640]{2,1,0:T(8,128)(2,1)} %get-tuple-element.123), calls=%async_computation | async-start | bytes 3276800 | tf_op jit(solution)/shard_map/cond/branch_0_fun/all_to_all | solution.py:430
  247.6 11.9 %collective-permute-start.13 = (f32[8,128]{1,0:T(8,128)S(1)}, f32[8,128]{1,0:T(8,128)S(1)}, u32[]{:S(2)}, u32[]{:S(2)}) collective-permute-start(f32[8,128]{1,0:T(8,128)S(1)} %add.279), channel_id=1, source_target_pairs={{0,4},{1,5},{2,6},{3,7},{4,0},{5,1},{6,2},{7,3},{8,12},{9,13},{10,... | collective-permute-start | bytes 12296 | tf_op jit(solution)/shard_map/cond/branch_0_fun/ppermute | solution.py:102
  (40 other events, 386.5 us)
where the time goes:
time: 266 us; the launch traced here: 265 us
  waiting for transfers between devices  113 us (42%)
  starting transfers between devices  56.4 us (21%)
  Pallas kernels  39.1 us (15%)
  local copies, waits for them, and re-layouts  24.6 us (9%)
  other arithmetic  23.3 us (9%)
  matrix products  6.16 us (2%)
    ppermute x6, waiting for transfers between devices, y_of(): return lax.ppermute(values, 'rep', Y_MATE)  56.3 us
    all_to_all x1, waiting for transfers between devices, gather_small(): lax.all_to_all(copies, 'fsdp', split_axis=0, concat_axis=0, tiled=True)  16.7 us
    pallas_call x1, Pallas kernels, first_scores(): pl.pallas_call(functools.partial(first_kernel, sizes=sizes, blocks=5), ou...  15.2 us
    ppermute x5, waiting for transfers between devices, along(): return lax.ppermute(values, 'fsdp', pairs)  14.5 us
    ppermute x4, waiting for transfers between devices, sum_in_turn(): values = values + lax.ppermute(values, axis, pairs)  14.5 us
    pallas_call x1, Pallas kernels, fresh_scores(): pl.pallas_call(fresh_kernel, grid=(2, 4), out_shape=jax.ShapeDtypeStruct(...  13.1 us
    pallas_call x1, Pallas kernels, grads_and_fresh(): pl.pallas_call(functools.partial(grad_kernel, rate, len(terms)), grid=(4,...  10.8 us
    all_to_all x1, starting transfers between devices, gather_small(): lax.all_to_all(copies, 'fsdp', split_axis=0, concat_axis=0, tiled=True)  8.97 us
  transfers between devices with their start and end apart: 35, of which 16 were waited for; matrix products, arithmetic and copies ran while one was open for 14% of the time, Pallas kernels for 5%

commit v1 on v0

--- a/solution.py
+++ b/solution.py
@@ -160,96 +160,90 @@
         sums_ref[chip] = jnp.broadcast_to(sums, sums_ref.shape[1:])
 
 
-def first_kernel(offsets_ref, *refs, sizes, blocks):
+def first_kernel(offsets_ref, *refs, sizes, blocks, half, carried):
     count = len(sizes)
     parts = refs[:count]
     own_w, mate_w, share_ref, spots_ref, bounds_ref = refs[count : count + 5]
-    pre_ref, sums_ref, kept_ref, given_ref, x_s, w_s, acc_s, in_sem, w_sem, out_sem = refs[count + 5 :]
+    outs = refs[count + 5 + carried :]
+    sums_ref, pre_ref, kept_ref, given_ref, x_s, w_s, acc_s, in_sem, w_sem, out_sem = outs
     wide = own_w.shape[2]
+    tile, width = x_s.shape
+    depth = width // blocks
     copies = []
     at = 0
     for index, size in enumerate(sizes):
         copies.append(pltpu.make_async_copy(parts[index], x_s.at[pl.ds(at, size)], in_sem.at[index]))
         at += size
-    weight_copies = []
     for core, source in enumerate((own_w, mate_w)):
         for j in range(4):
             where = pl.ds(pl.multiple_of(offsets_ref[core * 4 + j], 128), wide)
-            weight_copies.append(
-                pltpu.make_async_copy(source.at[j], w_s.at[:, where], w_sem.at[core * 4 + j])
+            copies.append(pltpu.make_async_copy(source.at[j], w_s.at[:, where], w_sem.at[core * 4 + j]))
+    for copy in copies:
+        copy.start()
+    acc_s[...] = jnp.zeros_like(acc_s)
+    for copy in copies:
+        copy.wait()
+    rows = pl.ds(half * tile, tile)
+    out_copies = []
+    for core, dest in enumerate((kept_ref, given_ref)):
+        for j in range(4):
+            where = pl.ds(pl.multiple_of(offsets_ref[core * 4 + j], 128), wide)
+            out_copies.append(
+                pltpu.make_async_copy(x_s.at[:, where], dest.at[j, rows], out_sem.at[core * 4 + j])
             )
-    for copy in weight_copies + copies:
-        copy.start()
-    for copy in weight_copies:
-        copy.wait()
-    total = x_s.shape[0]
-    tile = total // 2
-    depth = x_s.shape[1] // blocks
-    out_copies = []
-    waited = 0
-    at = 0
-    for half in range(2):
-        while at < (half + 1) * tile:
-            copies[waited].wait()
-            at += sizes[waited]
-            waited += 1
-        rows = pl.ds(half * tile, tile)
-        for core, dest in enumerate((kept_ref, given_ref)):
-            for j in range(4):
-                where = pl.ds(pl.multiple_of(offsets_ref[core * 4 + j], 128), wide)
-                out_copies.append(
-                    pltpu.make_async_copy(
-                        x_s.at[rows, where], dest.at[j, rows], out_sem.at[half * 8 + core * 4 + j]
-                    )
-                )
-                out_copies[-1].start()
-        acc_s[...] = jnp.zeros_like(acc_s)
-
-        @pl.loop(0, blocks)
-        def _(k):
-            where = pl.ds(pl.multiple_of(k * depth, 128), depth)
-            acc_s[...] += lax.dot_general(
-                w_s[:, where], x_s[rows, where], (((1,), (1,)), ((), ())), preferred_element_type=jnp.float32
-            )
-
-        pre = acc_s[...]
-        pre_ref[:, half * tile : (half + 1) * tile] = pre
-        step_sums(pre, share_ref[...], spots_ref[half * 2 : half * 2 + 2], bounds_ref, sums_ref, half * 2)
+            out_copies[-1].start()
+
+    @pl.loop(0, blocks)
+    def _(k):
+        where = pl.ds(pl.multiple_of(k * depth, 128), depth)
+        acc_s[...] += lax.dot_general(
+            w_s[:, where], x_s[:, where], (((1,), (1,)), ((), ())), preferred_element_type=jnp.float32
+        )
+
+    out_copies.append(pltpu.make_async_copy(acc_s, pre_ref.at[:, rows], out_sem.at[8]))
+    out_copies[-1].start()
+    step_sums(acc_s[...], share_ref[...], spots_ref[...], bounds_ref, sums_ref, 0)
     for copy in out_copies:
         copy.wait()
 
 
-def first_scores(parts, own_w, mate_w, share, spots, bounds, offsets):
+def first_scores(parts, own_w, mate_w, share, spots, bounds, offsets, half, carried=()):
     sizes = tuple(part.shape[0] for part in parts)
-    total = sum(sizes)
+    tile = sum(sizes)
     width = parts[0].shape[1]
     units, wide = own_w.shape[1:]
     anywhere = pl.BlockSpec(memory_space=pl.ANY)
     vmem = pl.BlockSpec(memory_space=pltpu.VMEM)
+    both = slice(half * 2, half * 2 + 2)
+    first_carried = 1 + len(parts) + 5
     return pl.pallas_call(
-        functools.partial(first_kernel, sizes=sizes, blocks=5),
+        functools.partial(first_kernel, sizes=sizes, blocks=5, half=half, carried=len(carried)),
         out_shape=(
-            jax.ShapeDtypeStruct((units, total), jnp.float32),
-            jax.ShapeDtypeStruct((4, bounds.shape[1], 128), jnp.float32),
-            jax.ShapeDtypeStruct((4, total, wide), jnp.bfloat16),
-            jax.ShapeDtypeStruct((4, total, wide), jnp.bfloat16),
+            jax.ShapeDtypeStruct((2, bounds.shape[1], 128), jnp.float32),
+            jax.ShapeDtypeStruct((units, 2 * tile), jnp.float32),
+            jax.ShapeDtypeStruct((4, 2 * tile, wide), jnp.bfloat16),
+            jax.ShapeDtypeStruct((4, 2 * tile, wide), jnp.bfloat16),
         ),
-        in_specs=[pl.BlockSpec(memory_space=pltpu.SMEM)] + [anywhere] * (len(parts) + 2) + [vmem] * 3,
-        out_specs=(vmem, vmem, anywhere, anywhere),
+        in_specs=[pl.BlockSpec(memory_space=pltpu.SMEM)]
+        + [anywhere] * (len(parts) + 2)
+        + [vmem] * 3
+        + [anywhere] * len(carried),
+        out_specs=(vmem, anywhere, anywhere, anywhere),
+        input_output_aliases={first_carried + i: 1 + i for i in range(len(carried))},
         scratch_shapes=[
-            pltpu.VMEM((total, width), jnp.bfloat16),
+            pltpu.VMEM((tile, width), jnp.bfloat16),
             pltpu.VMEM((units, width), jnp.bfloat16),
-            pltpu.VMEM((units, total // 2), jnp.float32),
+            pltpu.VMEM((units, tile), jnp.float32),
             pltpu.SemaphoreType.DMA((len(parts),)),
             pltpu.SemaphoreType.DMA((8,)),
-            pltpu.SemaphoreType.DMA((16,)),
+            pltpu.SemaphoreType.DMA((9,)),
         ],
         compiler_params=pltpu.CompilerParams(vmem_limit_bytes=VMEM_BYTES),
         cost_estimate=pl.CostEstimate(
-            flops=2 * units * width * total, bytes_accessed=4 * total * width, transcendentals=units * total
+            flops=2 * units * width * tile, bytes_accessed=4 * tile * width, transcendentals=units * tile
         ),
         name="first_scores",
-    )(offsets, *parts, own_w, mate_w, share, spots, bounds)
+    )(offsets, *parts, own_w, mate_w, share, spots[both], bounds[both], *carried)
 
 
 def fresh_kernel(kept_ref, given_ref, own_w, mate_w, share_ref, spots_ref, bounds_ref, sums_ref, acc_s):
@@ -409,7 +403,10 @@
     offsets = jnp.stack(blocks_at).astype(jnp.int32)
 
     def scored(parts, spots):
-        return first_scores(parts, own_head, mate_head, share, spots, bounds, offsets)
+        facts_of = (own_head, mate_head, share, spots, bounds, offsets)
+        low_sums, *carried = first_scores(parts[:6], *facts_of, 0)
+        high_sums, *carried = first_scores(parts[6:], *facts_of, 1, carried)
+        return (jnp.concatenate([low_sums, high_sums]), *carried)
 
     def pre_grad_of(pre, spots, step_error):
         errors = []
@@ -419,11 +416,11 @@
         return (jnp.concatenate(errors)[None, :] * share * silu_slope(pre)).astype(jnp.bfloat16)
 
     def rest_of(batches):
-        chip_sums = sum(sums[:, :, 0] for _, (_, sums, _, _) in batches)
+        chip_sums = sum(sums[:, :, 0] for _, (sums, _, _, _) in batches)
         step_score = of_chips(sum_over_chips(of_lines(chip_sums)))
         step_error = live_here * (step_score - labels_here)
         terms = []
-        for spots, (pre, _, kept, given) in batches:
+        for spots, (_, pre, kept, given) in batches:
             pre_grad = pre_grad_of(pre, spots, step_error)
             terms += [(pre_grad, kept), (core_swap(pre_grad), core_swap(given))]
         grads, own_fresh = grads_and_fresh(own_head, terms, rate)

time: 266 us -> 255 us (0.959)
  other arithmetic: 23.3 us -> 15.5 us
  local copies, waits for them, and re-layouts: 24.6 us -> 18.2 us
  Pallas kernels: 39.1 us -> 43 us
    ppermute x6, waiting for transfers between devices: 56.3 us -> 52 us  [y_of(): return lax.ppermute(values, 'rep', Y_MATE)]
    pallas_call x1 -> x2, Pallas kernels: 15.2 us -> 18.8 us  [first_scores(): pl.pallas_call(functools.partial(first_kernel, sizes=sizes, blocks=5, hal...]
    another operation x18 -> x7, local copies, waits for them, and re-layouts: 7.03 us -> 5.19 us
  transfers between devices with their start and end apart: 35 -> 35, of which waited for: 16 -> 17; matrix products, arithmetic and copies ran while one was open for 14% -> 10% of each run, Pallas kernels for 5% -> 9%
where the time goes in v1:
time: 255 us; the launch traced here: 254 us
  waiting for transfers between devices  113 us (44%)
  starting transfers between devices  56.3 us (22%)
  Pallas kernels  43 us (17%)
  local copies, waits for them, and re-layouts  18.2 us (7%)
  other arithmetic  15.5 us (6%)
  matrix products  6.16 us (2%)
    ppermute x6, waiting for transfers between devices, y_of(): return lax.ppermute(values, 'rep', Y_MATE)  52 us
    pallas_call x2, Pallas kernels, first_scores(): pl.pallas_call(functools.partial(first_kernel, sizes=sizes, blocks=5, hal...  18.8 us
    all_to_all x1, waiting for transfers between devices, gather_small(): lax.all_to_all(copies, 'fsdp', split_axis=0, concat_axis=0, tiled=True)  16.7 us
    ppermute x4, waiting for transfers between devices, sum_in_turn(): values = values + lax.ppermute(values, axis, pairs)  15.4 us
    ppermute x5, waiting for transfers between devices, along(): return lax.ppermute(values, 'fsdp', pairs)  14.5 us
    pallas_call x1, Pallas kernels, fresh_scores(): pl.pallas_call(fresh_kernel, grid=(2, 4), out_shape=jax.ShapeDtypeStruct(...  13.2 us
    pallas_call x1, Pallas kernels, grads_and_fresh(): pl.pallas_call(functools.partial(grad_kernel, rate, len(terms)), grid=(4,...  11 us
    ppermute x5, starting transfers between devices, along(): return lax.ppermute(values, 'fsdp', pairs)  8.97 us
  transfers between devices with their start and end apart: 35, of which 17 were waited for; matrix products, arithmetic and copies ran while one was open for 10% of the time, Pallas kernels for 9%

profile of v1, /device:TPU:0, one launch (start us, length us, event | category | flops | bytes accessed | tf_op | source)
XLA Modules:
  0.0 253.8 jit_solution(12968127181512406623)
XLA Ops:
  2.9 3.8 %multiply_reduce_fusion.2 = (f32[96]{0:T(128)S(1)}, f32[96,5120]{1,0:T(8,128)S(1)}) fusion(bf16[512,5120]{1,0:T(8,128)(2,1)} %bitcast.130, s32[512]{0:T(512)S(1)} %select_n.236, s32[96]{0:T(128)S(1)} %get-tuple-element.582), kind=kOutput, calls=%fused_computation.139 | convolution fusion | flops 505331616 | bytes 7211776 | tf_op jit(solution)/shard_map/dot_general | solution.py:356
  7.0 3.1 %collective-permute-start.47 = (bf16[96,5120]{1,0:T(8,128)(2,1)S(1)}, bf16[96,5120]{1,0:T(8,128)(2,1)S(1)}, u32[]{:S(2)}, u32[]{:S(2)}) collective-permute-start(bf16[96,5120]{1,0:T(8,128)(2,1)S(1)} %multiply_convert_fusion.5), channel_id=1, source_target_pairs={{0,2},{1,3},{2,0},{3,1},{4,6},{5,7},{6,4},{7,5},{8,10},{9,11},{10,... | collective-permute-start | bytes 2949128 | tf_op jit(solution)/shard_map/ppermute | solution.py:116
  14.1 3.2 %fusion.15.refs_0_ = bf16[384,5120]{1,0:T(8,128)(2,1)} fusion(bf16[384,5120]{1,0:T(8,128)(2,1)S(1)} %get-tuple-element.576, f32[5120]{0:T(1024)S(1)} %copy-done.17, f32[384]{0:T(512)S(1)} %add_rsqrt_fusion.2), kind=kLoop, calls=%fused_computation.134 | loop fusion | flops 7864320 | bytes 7886336 | tf_op jit(solution)/shard_map/convert_element_type | solution.py:25
  17.3 14.5 %collective-permute-done.47.refs_1_ = bf16[96,5120]{1,0:T(8,128)(2,1)S(1)} collective-permute-done((bf16[96,5120]{1,0:T(8,128)(2,1)S(1)}, bf16[96,5120]{1,0:T(8,128)(2,1)S(1)}, u32[]{:S(2)}, u32[]{:S(2)}) %collective-permute-start.47) | collective-permute-done | bytes 983072 | tf_op jit(solution)/shard_map/ppermute | solution.py:116
  39.2 8.9 %all-to-all-start.2 = ((f32[8,1,384]{2,1,0:T(1,128)}), f32[8,1,384]{2,1,0:T(1,128)S(1)}, u32[]{:S(2)}, u32[]{:S(2)}) async-start(f32[8,1,384]{2,1,0:T(1,128)} %broadcast_in_dim.585), calls=%async_computation.2 | async-start | bytes 24576 | tf_op jit(solution)/shard_map/all_to_all | solution.py:108
  48.1 16.7 %all-to-all-done.2 = f32[8,1,384]{2,1,0:T(1,128)S(1)} async-done(((f32[8,1,384]{2,1,0:T(1,128)}), f32[8,1,384]{2,1,0:T(1,128)S(1)}, u32[]{:S(2)}, u32[]{:S(2)}) %all-to-all-start.2) | async-done | bytes 12320 | tf_op jit(solution)/shard_map/all_to_all | solution.py:108
  73.2 3.5 %copy.60 = bf16[1280,640]{1,0:T(8,128)(2,1)} copy(bf16[1280,640]{0,1:T(8,128)(2,1)} %bitcast.135) | data formatting | bytes 3276800 | tf_op jit(solution)/shard_map/transpose | solution.py:375
  76.7 24.8 %collective-permute-done.53.refs_4_ = bf16[48,5120]{1,0:T(8,128)(2,1)S(1)} collective-permute-done((bf16[48,5120]{1,0:T(8,128)(2,1)}, bf16[48,5120]{1,0:T(8,128)(2,1)S(1)}, u32[]{:S(2)}, u32[]{:S(2)}) %collective-permute-start.53) | collective-permute-done | bytes 491552 | tf_op jit(solution)/shard_map/ppermute | solution.py:122
  101.5 4.4 %all-to-all-start.3 = ((bf16[4,320,640]{2,1,0:T(8,128)(2,1)}), bf16[4,320,640]{2,1,0:T(8,128)(2,1)}, u32[]{:S(2)}, u32[]{:S(2)}) async-start(bf16[4,320,640]{2,1,0:T(8,128)(2,1)} %bitcast.71), calls=%async_computation.3 | async-start | bytes 3276800 | tf_op jit(solution)/shard_map/all_to_all | solution.py:137
  114.4 27.2 %collective-permute-done.58.refs_3_ = bf16[48,5120]{1,0:T(8,128)(2,1)S(1)} collective-permute-done((bf16[48,5120]{1,0:T(8,128)(2,1)S(1)}, bf16[48,5120]{1,0:T(8,128)(2,1)S(1)}, u32[]{:S(2)}, u32[]{:S(2)}) %collective-permute-start.58) | collective-permute-done | bytes 491552 | tf_op jit(solution)/shard_map/ppermute | solution.py:122
  151.9 9.6 %first_scores.6 = (f32[2,128,128]{2,1,0:T(8,128)S(1)}, f32[320,1536]{1,0:T(8,128)}, bf16[4,1536,640]{2,1,0:T(8,128)(2,1)}, bf16[4,1536,640]{2,1,0:T(8,128)(2,1)}) custom-call(s32[8]{0:T(128)S(1)} %stack.160.offsets_ref, bf16[384,5120]{1,0:T(8,128)(2,1)} %fusion.15.refs_0_, bf16[96,5120]{1,0:T(8,128)(2,1)} %copy-done.12, bf16[96,5120]{1,0:T(8,128)(2,1)} %copy-done.6, ...), custom_call_target="tpu_custom_call" | custom-call | flops 2516582400 | bytes 15728640 | tf_op jit(solution)/shard_map/first_scores/pallas_call | solution.py:219
  163.1 9.2 %first_scores.7 = (f32[2,128,128]{2,1,0:T(8,128)S(1)}, f32[320,1536]{1,0:T(8,128)}, bf16[4,1536,640]{2,1,0:T(8,128)(2,1)}, bf16[4,1536,640]{2,1,0:T(8,128)(2,1)}) custom-call(s32[8]{0:T(128)S(1)} %stack.160.offsets_ref, bf16[96,5120]{1,0:T(8,128)(2,1)} %copy-done.2, ...), custom_call_target="tpu_custom_call", output_to_operand_aliasing={{1}: (16, {}), {2}: (17, {}), {3}: (18, {})} | custom-call | flops 2516582400 | bytes 15728640 | tf_op jit(solution)/shard_map/first_scores/pallas_call | solution.py:219
  172.5 81.4 %conditional.3 = (f32[16,8]{0,1:T(8,128)}, f32[640,1280]{1,0:T(8,128)}) conditional(s32[]{:T(128)} %convert_element_type.116, (f32[8,16]{1,0:T(8,128)S(1)}, s32[]{:T(128)}, pred[8]{0:T(512)(128)(4,1)S(1)}, f32[4,1,384]{2,1,0:T(1,128)S(1)}, f32[4,128,1]{1,0,2:T(4,128)S(1)}, /*index=5*/f32[4,128,1]{1,0,2:T(4,128)S(1)}, ...), branch_computations={%region_23.33_spmd, %region_33.49_spmd} | conditional | flops 15953286144 | bytes 220147200
  178.0 2.4 collective-permute-done.2
  185.1 2.8 %collective-permute-done.5 = f32[8,128]{1,0:T(8,128)S(1)} collective-permute-done((f32[8,128]{1,0:T(8,128)S(1)}, f32[8,128]{1,0:T(8,128)S(1)}, u32[]{:S(2)}, u32[]{:S(2)}) %collective-permute-start.5) | collective-permute-done | bytes 4128 | tf_op jit(solution)/shard_map/cond/branch_0_fun/ppermute | solution.py:92
  190.9 2.6 %collective-permute-done.6.refs_3_ = bf16[320,1536]{1,0:T(8,128)(2,1)S(1)} collective-permute-done((bf16[320,1536]{1,0:T(8,128)(2,1)S(1)}, bf16[320,1536]{1,0:T(8,128)(2,1)S(1)}, u32[]{:S(2)}, u32[]{:S(2)}) %collective-permute-start.6) | collective-permute-done | bytes 983072 | tf_op jit(solution)/shard_map/cond/branch_0_fun/ppermute | solution.py:97
  193.4 11.0 %grads_and_fresh.2 = (bf16[4,320,640]{2,1,0:T(8,128)(2,1)}, bf16[4,320,640]{2,1,0:T(8,128)(2,1)}) custom-call(bf16[4,320,640]{2,1,0:T(8,128)(2,1)} %get-tuple-element.109.refs_0_, bf16[320,1536]{1,0:T(8,128)(2,1)S(1)} %multiply_convert_fusion.refs_1_, bf16[4,1536,640]{2,1,0:T(8,128)(2,1)} %get-tuple-element.107.refs_2_.kept_ref, ...), custom_call_target="tpu_custom_call" | custom-call | flops 5033164800 | bytes 15728640 | tf_op jit(solution)/shard_map/cond/branch_0_fun/grads_and_fresh/pallas_call | solution.py:321
  204.5 4.4 %all-to-all-start = ((bf16[4,320,640]{2,1,0:T(8,128)(2,1)}), bf16[4,320,640]{2,1,0:T(8,128)(2,1)}, u32[]{:S(2)}, u32[]{:S(2)}) async-start(bf16[4,320,640]{2,1,0:T(8,128)(2,1)} %get-tuple-element.123), calls=%async_computation | async-start | bytes 3276800 | tf_op jit(solution)/shard_map/cond/branch_0_fun/all_to_all | solution.py:427
  210.4 13.2 %fresh_scores.3 = f32[4,128,128]{2,1,0:T(8,128)S(1)} custom-call(bf16[4,1536,640]{2,1,0:T(8,128)(2,1)} %get-tuple-element.107.refs_2_.kept_ref, bf16[4,1536,640]{2,1,0:T(8,128)(2,1)} %get-tuple-element.108.given_ref, bf16[4,320,640]{2,1,0:T(8,128)(2,1)} %get-tuple-element.121.own_w, bf16[4,320,640]{2,1,0:T(8,128)(2,1)} %copy-done.8, ...), custom_call_target="tpu_custom_call" | custom-call | flops 5033164800 | bytes 15728640 | tf_op jit(solution)/shard_map/cond/branch_0_fun/fresh_scores/pallas_call | solution.py:276
  225.7 3.0 %collective-permute-done.10 = f32[8,128]{1,0:T(8,128)S(1)} collective-permute-done((f32[8,128]{1,0:T(8,128)S(1)}, f32[8,128]{1,0:T(8,128)S(1)}, u32[]{:S(2)}, u32[]{:S(2)}) %collective-permute-start.10) | collective-permute-done | bytes 4128 | tf_op jit(solution)/shard_map/cond/branch_0_fun/ppermute | solution.py:102
  229.3 3.1 %collective-permute-done.11 = f32[8,128]{1,0:T(8,128)S(1)} collective-permute-done((f32[8,128]{1,0:T(8,128)S(1)}, f32[8,128]{1,0:T(8,128)S(1)}, u32[]{:S(2)}, u32[]{:S(2)}) %collective-permute-start.11) | collective-permute-done | bytes 4128 | tf_op jit(solution)/shard_map/cond/branch_0_fun/ppermute | solution.py:102
  236.4 4.5 %collective-permute-start.13 = (f32[8,128]{1,0:T(8,128)S(1)}, f32[8,128]{1,0:T(8,128)S(1)}, u32[]{:S(2)}, u32[]{:S(2)}) collective-permute-start(f32[8,128]{1,0:T(8,128)S(1)} %add.279), channel_id=1, source_target_pairs={{0,4},{1,5},{2,6},{3,7},{4,0},{5,1},{6,2},{7,3},{8,12},{9,13},{10,... | collective-permute-start | bytes 12296 | tf_op jit(solution)/shard_map/cond/branch_0_fun/ppermute | solution.py:102
  241.0 7.3 %collective-permute-done.13 = f32[8,128]{1,0:T(8,128)S(1)} collective-permute-done((f32[8,128]{1,0:T(8,128)S(1)}, f32[8,128]{1,0:T(8,128)S(1)}, u32[]{:S(2)}, u32[]{:S(2)}) %collective-permute-start.13) | collective-permute-done | bytes 4128 | tf_op jit(solution)/shard_map/cond/branch_0_fun/ppermute | solution.py:102
  250.9 3.0 %copy.78 = f32[640,1280]{1,0:T(8,128)} copy(f32[640,1280]{0,1:T(8,128)S(1)} %convert_bitcast_fusion) | data formatting | bytes 6553600 | tf_op jit(solution)/shard_map/conditional.1
  (176 shorter events, 65.7 us)
Async XLA Ops:
  7.0 24.8 %collective-permute-start.47 = (bf16[96,5120]{1,0:T(8,128)(2,1)S(1)}, bf16[96,5120]{1,0:T(8,128)(2,1)S(1)}, u32[]{:S(2)}, u32[]{:S(2)}) collective-permute-start(bf16[96,5120]{1,0:T(8,128)(2,1)S(1)} %multiply_convert_fusion.5), channel_id=1, source_target_pairs={{0,2},{1,3},{2,0},{3,1},{4,6},{5,7},{6,4},{7,5},{8,10},{9,11},{10,... | collective-permute-start | bytes 2949128 | tf_op jit(solution)/shard_map/ppermute | solution.py:116
  10.0 21.8 %collective-permute-start.48 = (bf16[96,5120]{1,0:T(8,128)(2,1)S(1)}, bf16[96,5120]{1,0:T(8,128)(2,1)}, u32[]{:S(2)}, u32[]{:S(2)}) collective-permute-start(bf16[96,5120]{1,0:T(8,128)(2,1)S(1)} %multiply_convert_fusion.5), channel_id=1, source_target_pairs={{2,4},{3,5},{4,2},{5,3},{10,12},{11,13},{12,10},{13,11},{18,20},{1... | collective-permute-start | bytes 2949128 | tf_op jit(solution)/shard_map/ppermute | solution.py:116
  31.8 33.0 %collective-permute-start.49 = (bf16[96,5120]{1,0:T(8,128)(2,1)S(1)}, bf16[96,5120]{1,0:T(8,128)(2,1)S(1)}, u32[]{:S(2)}, u32[]{:S(2)}) collective-permute-start(bf16[96,5120]{1,0:T(8,128)(2,1)S(1)} %collective-permute-done.47.refs_1_), channel_id=1, source_target_pairs={{0,8},{8,0},{16,24},{24,16},{1,9},{9,1},{17,25},{25,17},{2,10},{10... | collective-permute-start | bytes 2949128 | tf_op jit(solution)/shard_map/ppermute | solution.py:119
  33.5 31.3 %collective-permute-start.50 = (bf16[96,5120]{1,0:T(8,128)(2,1)S(1)}, bf16[96,5120]{1,0:T(8,128)(2,1)S(1)}, u32[]{:S(2)}, u32[]{:S(2)}) collective-permute-start(bf16[96,5120]{1,0:T(8,128)(2,1)S(1)} %collective-permute-done.47.refs_1_), channel_id=1, source_target_pairs={{0,16},{8,24},{16,0},{24,8},{1,17},{9,25},{17,1},{25,9},{2,18},{10... | collective-permute-start | bytes 2949128 | tf_op jit(solution)/shard_map/ppermute | solution.py:122
  35.0 29.8 %collective-permute-start.52 = (bf16[96,5120]{1,0:T(8,128)(2,1)S(1)}, bf16[96,5120]{1,0:T(8,128)(2,1)}, u32[]{:S(2)}, u32[]{:S(2)}) collective-permute-start(bf16[96,5120]{1,0:T(8,128)(2,1)S(1)} %collective-permute-done.47.refs_1_), channel_id=1, source_target_pairs={{2,4},{3,5},{4,2},{5,3},{10,12},{11,13},{12,10},{13,11},{18,20},{1... | collective-permute-start | bytes 2949128 | tf_op jit(solution)/shard_map/ppermute | solution.py:116
  36.7 28.2 %collective-permute-start.51 = (bf16[96,5120]{1,0:T(8,128)(2,1)}, bf16[96,5120]{1,0:T(8,128)(2,1)}, u32[]{:S(2)}, u32[]{:S(2)}) collective-permute-start(bf16[96,5120]{1,0:T(8,128)(2,1)} %collective-permute-done.48), channel_id=1, source_target_pairs={{2,0},{3,1},{4,6},{5,7},{10,8},{11,9},{12,14},{13,15},{18,16},{19,... | collective-permute-start | bytes 2949128 | tf_op jit(solution)/shard_map/ppermute | solution.py:116
  39.2 25.5 %all-to-all-start.2 = ((f32[8,1,384]{2,1,0:T(1,128)}), f32[8,1,384]{2,1,0:T(1,128)S(1)}, u32[]{:S(2)}, u32[]{:S(2)}) async-start(f32[8,1,384]{2,1,0:T(1,128)} %broadcast_in_dim.585), calls=%async_computation.2 | async-start | bytes 24576 | tf_op jit(solution)/shard_map/all_to_all | solution.py:108
  66.8 34.6 %collective-permute-start.55 = (bf16[96,5120]{1,0:T(8,128)(2,1)S(1)}, bf16[96,5120]{1,0:T(8,128)(2,1)}, u32[]{:S(2)}, u32[]{:S(2)}) collective-permute-start(bf16[96,5120]{1,0:T(8,128)(2,1)S(1)} %broadcast_select_fusion.3.refs_0_), channel_id=1, source_target_pairs={{0,8},{8,0},{16,24},{24,16},{1,9},{9,1},{17,25},{25,17},{2,10},{10... | collective-permute-start | bytes 2949128 | tf_op jit(solution)/shard_map/ppermute | solution.py:119
  67.5 34.0 %collective-permute-start.56 = (bf16[96,5120]{1,0:T(8,128)(2,1)S(1)}, bf16[96,5120]{1,0:T(8,128)(2,1)}, u32[]{:S(2)}, u32[]{:S(2)}) collective-permute-start(bf16[96,5120]{1,0:T(8,128)(2,1)S(1)} %broadcast_select_fusion.3.refs_0_), channel_id=1, source_target_pairs={{0,16},{8,24},{16,0},{24,8},{1,17},{9,25},{17,1},{25,9},{2,18},{10... | collective-permute-start | bytes 2949128 | tf_op jit(solution)/shard_map/ppermute | solution.py:122
  68.0 33.5 %collective-permute-start.57 = (bf16[96,5120]{1,0:T(8,128)(2,1)}, bf16[96,5120]{1,0:T(8,128)(2,1)}, u32[]{:S(2)}, u32[]{:S(2)}) collective-permute-start(bf16[96,5120]{1,0:T(8,128)(2,1)} %collective-permute-done.52), channel_id=1, source_target_pairs={{2,0},{3,1},{4,6},{5,7},{10,8},{11,9},{12,14},{13,15},{18,16},{19,... | collective-permute-start | bytes 2949128 | tf_op jit(solution)/shard_map/ppermute | solution.py:116
  70.1 31.4 %collective-permute-start.53 = (bf16[48,5120]{1,0:T(8,128)(2,1)}, bf16[48,5120]{1,0:T(8,128)(2,1)S(1)}, u32[]{:S(2)}, u32[]{:S(2)}) collective-permute-start(bf16[48,5120]{1,0:T(8,128)(2,1)} %slice.293), channel_id=1, source_target_pairs={{0,16},{8,24},{16,0},{24,8},{1,17},{9,25},{17,1},{25,9},{2,18},{10... | collective-permute-start | bytes 1474568 | tf_op jit(solution)/shard_map/ppermute | solution.py:122
  71.6 29.8 %collective-permute-start.54 = (bf16[48,5120]{1,0:T(8,128)(2,1)S(1)}, bf16[48,5120]{1,0:T(8,128)(2,1)S(1)}, u32[]{:S(2)}, u32[]{:S(2)}) collective-permute-start(bf16[48,5120]{1,0:T(8,128)(2,1)S(1)} %slice.294), channel_id=1, source_target_pairs={{0,8},{8,0},{16,24},{24,16},{1,9},{9,1},{17,25},{25,17},{2,10},{10... | collective-permute-start | bytes 1474568 | tf_op jit(solution)/shard_map/ppermute | solution.py:119
  101.5 42.3 %all-to-all-start.3 = ((bf16[4,320,640]{2,1,0:T(8,128)(2,1)}), bf16[4,320,640]{2,1,0:T(8,128)(2,1)}, u32[]{:S(2)}, u32[]{:S(2)}) async-start(bf16[4,320,640]{2,1,0:T(8,128)(2,1)} %bitcast.71), calls=%async_computation.3 | async-start | bytes 3276800 | tf_op jit(solution)/shard_map/all_to_all | solution.py:137
  107.2 34.4 %collective-permute-start.60 = (bf16[96,5120]{1,0:T(8,128)(2,1)S(1)}, bf16[96,5120]{1,0:T(8,128)(2,1)}, u32[]{:S(2)}, u32[]{:S(2)}) collective-permute-start(bf16[96,5120]{1,0:T(8,128)(2,1)S(1)} %broadcast_select_fusion.2.refs_5_), channel_id=1, source_target_pairs={{0,8},{8,0},{16,24},{24,16},{1,9},{9,1},{17,25},{25,17},{2,10},{10... | collective-permute-start | bytes 2949128 | tf_op jit(solution)/shard_map/ppermute | solution.py:119
  108.8 32.9 %collective-permute-start.61 = (bf16[96,5120]{1,0:T(8,128)(2,1)S(1)}, bf16[96,5120]{1,0:T(8,128)(2,1)}, u32[]{:S(2)}, u32[]{:S(2)}) collective-permute-start(bf16[96,5120]{1,0:T(8,128)(2,1)S(1)} %broadcast_select_fusion.2.refs_5_), channel_id=1, source_target_pairs={{0,16},{8,24},{16,0},{24,8},{1,17},{9,25},{17,1},{25,9},{2,18},{10... | collective-permute-start | bytes 2949128 | tf_op jit(solution)/shard_map/ppermute | solution.py:122
  110.3 31.3 %collective-permute-start.58 = (bf16[48,5120]{1,0:T(8,128)(2,1)S(1)}, bf16[48,5120]{1,0:T(8,128)(2,1)S(1)}, u32[]{:S(2)}, u32[]{:S(2)}) collective-permute-start(bf16[48,5120]{1,0:T(8,128)(2,1)S(1)} %slice.295), channel_id=1, source_target_pairs={{0,16},{8,24},{16,0},{24,8},{1,17},{9,25},{17,1},{25,9},{2,18},{10... | collective-permute-start | bytes 1474568 | tf_op jit(solution)/shard_map/ppermute | solution.py:122
  113.8 27.9 %collective-permute-start.59 = (bf16[48,5120]{1,0:T(8,128)(2,1)}, bf16[48,5120]{1,0:T(8,128)(2,1)S(1)}, u32[]{:S(2)}, u32[]{:S(2)}) collective-permute-start(bf16[48,5120]{1,0:T(8,128)(2,1)} %slice.296), channel_id=1, source_target_pairs={{0,8},{8,0},{16,24},{24,16},{1,9},{9,1},{17,25},{25,17},{2,10},{10... | collective-permute-start | bytes 1474568 | tf_op jit(solution)/shard_map/ppermute | solution.py:119
  143.8 8.1 %collective-permute-start.62 = (bf16[4,320,640]{2,1,0:T(8,128)(2,1)}, bf16[4,320,640]{2,1,0:T(8,128)(2,1)}, u32[]{:S(2)}, u32[]{:S(2)}) collective-permute-start(bf16[4,320,640]{2,1,0:T(8,128)(2,1)} %all-to-all-done.3.refs_6_.refs_10_), channel_id=1, source_target_pairs={{0,1},{1,0},{2,3},{3,2},{4,5},{5,4},{6,7},{7,6},{8,9},{9,8},{10,11... | collective-permute-start | bytes 4915208 | tf_op jit(solution)/shard_map/ppermute | solution.py:97
  147.0 14.5 %collective-permute-start.63 = (bf16[48,5120]{1,0:T(8,128)(2,1)S(1)}, bf16[48,5120]{1,0:T(8,128)(2,1)S(1)}, u32[]{:S(2)}, u32[]{:S(2)}) collective-permute-start(bf16[48,5120]{1,0:T(8,128)(2,1)S(1)} %slice.299), channel_id=1, source_target_pairs={{0,16},{8,24},{16,0},{24,8},{1,17},{9,25},{17,1},{25,9},{2,18},{10... | collective-permute-start | bytes 1474568 | tf_op jit(solution)/shard_map/ppermute | solution.py:122
  149.4 13.6 %collective-permute-start.64 = (bf16[48,5120]{1,0:T(8,128)(2,1)}, bf16[48,5120]{1,0:T(8,128)(2,1)}, u32[]{:S(2)}, u32[]{:S(2)}) collective-permute-start(bf16[48,5120]{1,0:T(8,128)(2,1)} %slice.300), channel_id=1, source_target_pairs={{0,8},{8,0},{16,24},{24,16},{1,9},{9,1},{17,25},{25,17},{2,10},{10... | collective-permute-start | bytes 1474568 | tf_op jit(solution)/shard_map/ppermute | solution.py:119
  172.6 20.8 %collective-permute-start.7 = (bf16[4,1536,640]{2,1,0:T(8,128)(2,1)}, bf16[4,1536,640]{2,1,0:T(8,128)(2,1)}, u32[]{:S(2)}, u32[]{:S(2)}) collective-permute-start(bf16[4,1536,640]{2,1,0:T(8,128)(2,1)} %get-tuple-element.108.given_ref), channel_id=1, source_target_pairs={{0,1},{1,0},{2,3},{3,2},{4,5},{5,4},{6,7},{7,6},{8,9},{9,8},{10,11... | collective-permute-start | bytes 23592968 | tf_op jit(solution)/shard_map/cond/branch_0_fun/ppermute | solution.py:97
  182.5 5.4 %collective-permute-start.5 = (f32[8,128]{1,0:T(8,128)S(1)}, f32[8,128]{1,0:T(8,128)S(1)}, u32[]{:S(2)}, u32[]{:S(2)}) collective-permute-start(f32[8,128]{1,0:T(8,128)S(1)} %add_add_fusion.1), channel_id=1, source_target_pairs={{0,6},{1,7},{2,4},{3,5},{4,2},{5,3},{6,0},{7,1},{8,14},{9,15},{10,... | collective-permute-start | bytes 12296 | tf_op jit(solution)/shard_map/cond/branch_0_fun/ppermute | solution.py:92
  204.5 44.7 %all-to-all-start = ((bf16[4,320,640]{2,1,0:T(8,128)(2,1)}), bf16[4,320,640]{2,1,0:T(8,128)(2,1)}, u32[]{:S(2)}, u32[]{:S(2)}) async-start(bf16[4,320,640]{2,1,0:T(8,128)(2,1)} %get-tuple-element.123), calls=%async_computation | async-start | bytes 3276800 | tf_op jit(solution)/shard_map/cond/branch_0_fun/all_to_all | solution.py:427
  236.4 11.9 %collective-permute-start.13 = (f32[8,128]{1,0:T(8,128)S(1)}, f32[8,128]{1,0:T(8,128)S(1)}, u32[]{:S(2)}, u32[]{:S(2)}) collective-permute-start(f32[8,128]{1,0:T(8,128)S(1)} %add.279), channel_id=1, source_target_pairs={{0,4},{1,5},{2,6},{3,7},{4,0},{5,1},{6,2},{7,3},{8,12},{9,13},{10,... | collective-permute-start | bytes 12296 | tf_op jit(solution)/shard_map/cond/branch_0_fun/ppermute | solution.py:102
  (26 other events, 278.6 us)

commit v2 on v1

--- a/solution.py
+++ b/solution.py
@@ -130,13 +130,18 @@
     ax, ay, b_out, c_in = together(second)
     b = jnp.where(inner, b_in, b_out)
     c_out = along(c_in, OUTWARD)
+    if weights is not None:
+        weights, ax = together((weights, ax))
+        weights = lax.all_to_all(
+            jnp.transpose(weights).reshape(4, -1, weights.shape[0]),
+            "fsdp",
+            0,
+            0,
+            axis_index_groups=[[0, 2, 4, 6], [1, 3, 5, 7]],
+            tiled=True,
+        )
     a_low, a_high, bx, by = together((y_of(ax[:half]), x_of(ay[half:]), x_of(b), y_of(b)))
     c_out, bx = together((c_out, bx))
-    if weights is not None:
-        weights, c_out = together((weights, c_out))
-        weights = lax.all_to_all(
-            weights, "fsdp", 0, 0, axis_index_groups=[[0, 2, 4, 6], [1, 3, 5, 7]], tiled=True
-        )
     c = jnp.where(inner, c_in, c_out)
     fourth = (y_of(bx[:half]), x_of(by[half:]), x_of(c), y_of(c))
     if weights is not None:
@@ -147,20 +152,19 @@
     return parts, weights, facts
 
 
-def step_sums(pre, share, spots, bounds_ref, sums_ref, first):
+def step_sums(pre, share, spots, bounds_ref, sums_ref):
     score = jnp.sum(pre * jax.nn.sigmoid(pre) * share, axis=0, keepdims=True)
     span = spots.shape[2]
-    for at in range(2):
-        chip = first + at
+    for at in range(spots.shape[0]):
         here = spots[at]
-        low = bounds_ref[chip, :, 0:1]
-        high = bounds_ref[chip, :, 1:2]
+        low = bounds_ref[at, :, 0:1]
+        high = bounds_ref[at, :, 1:2]
         inside = (here >= low) & (here < high)
         sums = jnp.sum(jnp.where(inside, score[:, at * span : (at + 1) * span], 0.0), axis=1, keepdims=True)
-        sums_ref[chip] = jnp.broadcast_to(sums, sums_ref.shape[1:])
-
-
-def first_kernel(offsets_ref, *refs, sizes, blocks, half, carried):
+        sums_ref[at] = jnp.broadcast_to(sums, sums_ref.shape[1:])
+
+
+def first_kernel(offsets_ref, *refs, sizes, blocks, first, carried):
     count = len(sizes)
     parts = refs[:count]
     own_w, mate_w, share_ref, spots_ref, bounds_ref = refs[count : count + 5]
@@ -183,7 +187,7 @@
     acc_s[...] = jnp.zeros_like(acc_s)
     for copy in copies:
         copy.wait()
-    rows = pl.ds(half * tile, tile)
+    rows = pl.ds(first, tile)
     out_copies = []
     for core, dest in enumerate((kept_ref, given_ref)):
         for j in range(4):
@@ -202,27 +206,28 @@
 
     out_copies.append(pltpu.make_async_copy(acc_s, pre_ref.at[:, rows], out_sem.at[8]))
     out_copies[-1].start()
-    step_sums(acc_s[...], share_ref[...], spots_ref[...], bounds_ref, sums_ref, 0)
+    step_sums(acc_s[...], share_ref[...], spots_ref[...], bounds_ref, sums_ref)
     for copy in out_copies:
         copy.wait()
 
 
-def first_scores(parts, own_w, mate_w, share, spots, bounds, offsets, half, carried=()):
+def first_scores(parts, own_w, mate_w, share, spots, bounds, offsets, first, chips, carried=()):
     sizes = tuple(part.shape[0] for part in parts)
     tile = sum(sizes)
     width = parts[0].shape[1]
     units, wide = own_w.shape[1:]
     anywhere = pl.BlockSpec(memory_space=pl.ANY)
     vmem = pl.BlockSpec(memory_space=pltpu.VMEM)
-    both = slice(half * 2, half * 2 + 2)
+    here = slice(first, first + chips)
+    total = tile // chips * 4
     first_carried = 1 + len(parts) + 5
     return pl.pallas_call(
-        functools.partial(first_kernel, sizes=sizes, blocks=5, half=half, carried=len(carried)),
+        functools.partial(first_kernel, sizes=sizes, blocks=5, first=first * (tile // chips), carried=len(carried)),
         out_shape=(
-            jax.ShapeDtypeStruct((2, bounds.shape[1], 128), jnp.float32),
-            jax.ShapeDtypeStruct((units, 2 * tile), jnp.float32),
-            jax.ShapeDtypeStruct((4, 2 * tile, wide), jnp.bfloat16),
-            jax.ShapeDtypeStruct((4, 2 * tile, wide), jnp.bfloat16),
+            jax.ShapeDtypeStruct((chips, bounds.shape[1], 128), jnp.float32),
+            jax.ShapeDtypeStruct((units, total), jnp.float32),
+            jax.ShapeDtypeStruct((4, total, wide), jnp.bfloat16),
+            jax.ShapeDtypeStruct((4, total, wide), jnp.bfloat16),
         ),
         in_specs=[pl.BlockSpec(memory_space=pltpu.SMEM)]
         + [anywhere] * (len(parts) + 2)
@@ -243,7 +248,7 @@
             flops=2 * units * width * tile, bytes_accessed=4 * tile * width, transcendentals=units * tile
         ),
         name="first_scores",
-    )(offsets, *parts, own_w, mate_w, share, spots[both], bounds[both], *carried)
+    )(offsets, *parts, own_w, mate_w, share, spots[here], bounds[here], *carried)
 
 
 def fresh_kernel(kept_ref, given_ref, own_w, mate_w, share_ref, spots_ref, bounds_ref, sums_ref, acc_s):
@@ -263,7 +268,7 @@
 
     @pl.when(k == 3)
     def _():
-        step_sums(acc_s[...], share_ref[...], spots_ref[...], bounds_ref, sums_ref, 0)
+        step_sums(acc_s[...], share_ref[...], spots_ref[...], bounds_ref, sums_ref)
 
 
 def fresh_scores(kept, given, own_w, mate_w, share, spots, bounds):
@@ -372,8 +377,7 @@
         [counts.reshape(-1), labels.astype(jnp.float32).reshape(-1), slot_of.astype(jnp.float32)]
     )
     facts = jnp.pad(facts, (0, 384 - facts.shape[0]))
-    head_t = jnp.transpose(head_in).reshape(4, units, wide)
-    main_parts, main_spots, own_head, facts_all = gathered(0, LOCAL, head_t, facts)
+    main_parts, main_spots, own_head, facts_all = gathered(0, LOCAL, head_in, facts)
     steps = row_count * STEPS
     counts_all = facts_all[:, :steps]
     labels_all = facts_all[:, steps : 2 * steps]
@@ -404,9 +408,9 @@
 
     def scored(parts, spots):
         facts_of = (own_head, mate_head, share, spots, bounds, offsets)
-        low_sums, *carried = first_scores(parts[:6], *facts_of, 0)
-        high_sums, *carried = first_scores(parts[6:], *facts_of, 1, carried)
-        return (jnp.concatenate([low_sums, high_sums]), *carried)
+        near_sums, *carried = first_scores(parts[:6], *facts_of, 0, 2)
+        last_sums, *carried = first_scores(parts[6:], *facts_of, 2, 2, carried)
+        return (jnp.concatenate([near_sums, last_sums]), *carried)
 
     def pre_grad_of(pre, spots, step_error):
         errors = []

time: 255 us -> 248 us (0.973)
  waiting for transfers between devices: 113 us -> 103 us
    ppermute x6, waiting for transfers between devices: 52 us -> 45.4 us  [y_of(): return lax.ppermute(values, 'rep', Y_MATE)]
where the time goes in v2:
time: 248 us; the launch traced here: 247 us
  waiting for transfers between devices  103 us (42%)
  starting transfers between devices  58.3 us (24%)
  Pallas kernels  43 us (17%)
  local copies, waits for them, and re-layouts  18.2 us (7%)
  other arithmetic  15.5 us (6%)
  matrix products  6.16 us (2%)
    ppermute x6, waiting for transfers between devices, y_of(): return lax.ppermute(values, 'rep', Y_MATE)  45.4 us
    pallas_call x2, Pallas kernels, first_scores(): pl.pallas_call(functools.partial(first_kernel, sizes=sizes, blocks=5, fir...  18.8 us
    all_to_all x1, waiting for transfers between devices, gather_small(): lax.all_to_all(copies, 'fsdp', split_axis=0, concat_axis=0, tiled=True)  16.7 us
    ppermute x5, waiting for transfers between devices, along(): return lax.ppermute(values, 'fsdp', pairs)  16.6 us
    ppermute x4, waiting for transfers between devices, sum_in_turn(): values = values + lax.ppermute(values, axis, pairs)  14.1 us
    pallas_call x1, Pallas kernels, fresh_scores(): pl.pallas_call(fresh_kernel, grid=(2, 4), out_shape=jax.ShapeDtypeStruct(...  13.2 us
    pallas_call x1, Pallas kernels, grads_and_fresh(): pl.pallas_call(functools.partial(grad_kernel, rate, len(terms)), grid=(4,...  11 us
    ppermute x5, starting transfers between devices, along(): return lax.ppermute(values, 'fsdp', pairs)  8.97 us
  transfers between devices with their start and end apart: 35, of which 17 were waited for; matrix products, arithmetic and copies ran while one was open for 10% of the time, Pallas kernels for 9%

profile of v2, /device:TPU:0, one launch (start us, length us, event | category | flops | bytes accessed | tf_op | source)
XLA Modules:
  0.0 246.7 jit_solution(14816116980768120102)
XLA Ops:
  2.9 3.8 %multiply_reduce_fusion.2 = (f32[96]{0:T(128)S(1)}, f32[96,5120]{1,0:T(8,128)S(1)}) fusion(bf16[512,5120]{1,0:T(8,128)(2,1)} %bitcast.130, s32[512]{0:T(512)S(1)} %select_n.236, s32[96]{0:T(128)S(1)} %get-tuple-element.582), kind=kOutput, calls=%fused_computation.139 | convolution fusion | flops 505331616 | bytes 7211776 | tf_op jit(solution)/shard_map/dot_general | solution.py:361
  7.0 3.1 %collective-permute-start.47 = (bf16[96,5120]{1,0:T(8,128)(2,1)S(1)}, bf16[96,5120]{1,0:T(8,128)(2,1)S(1)}, u32[]{:S(2)}, u32[]{:S(2)}) collective-permute-start(bf16[96,5120]{1,0:T(8,128)(2,1)S(1)} %multiply_convert_fusion.5), channel_id=1, source_target_pairs={{0,2},{1,3},{2,0},{3,1},{4,6},{5,7},{6,4},{7,5},{8,10},{9,11},{10,... | collective-permute-start | bytes 2949128 | tf_op jit(solution)/shard_map/ppermute | solution.py:116
  14.1 3.2 %fusion.15.refs_0_ = bf16[384,5120]{1,0:T(8,128)(2,1)} fusion(bf16[384,5120]{1,0:T(8,128)(2,1)S(1)} %get-tuple-element.576, f32[5120]{0:T(1024)S(1)} %copy-done.17, f32[384]{0:T(512)S(1)} %add_rsqrt_fusion.2), kind=kLoop, calls=%fused_computation.134 | loop fusion | flops 7864320 | bytes 7886336 | tf_op jit(solution)/shard_map/convert_element_type | solution.py:25
  17.3 14.5 %collective-permute-done.47.refs_1_ = bf16[96,5120]{1,0:T(8,128)(2,1)S(1)} collective-permute-done((bf16[96,5120]{1,0:T(8,128)(2,1)S(1)}, bf16[96,5120]{1,0:T(8,128)(2,1)S(1)}, u32[]{:S(2)}, u32[]{:S(2)}) %collective-permute-start.47) | collective-permute-done | bytes 983072 | tf_op jit(solution)/shard_map/ppermute | solution.py:116
  39.2 8.9 %all-to-all-start.2 = ((f32[8,1,384]{2,1,0:T(1,128)}), f32[8,1,384]{2,1,0:T(1,128)S(1)}, u32[]{:S(2)}, u32[]{:S(2)}) async-start(f32[8,1,384]{2,1,0:T(1,128)} %broadcast_in_dim.585), calls=%async_computation.2 | async-start | bytes 24576 | tf_op jit(solution)/shard_map/all_to_all | solution.py:108
  48.1 16.7 %all-to-all-done.2 = f32[8,1,384]{2,1,0:T(1,128)S(1)} async-done(((f32[8,1,384]{2,1,0:T(1,128)}), f32[8,1,384]{2,1,0:T(1,128)S(1)}, u32[]{:S(2)}, u32[]{:S(2)}) %all-to-all-start.2) | async-done | bytes 12320 | tf_op jit(solution)/shard_map/all_to_all | solution.py:108
  73.2 3.5 %copy.60 = bf16[1280,640]{1,0:T(8,128)(2,1)} copy(bf16[1280,640]{0,1:T(8,128)(2,1)} %bitcast.135) | data formatting | bytes 3276800 | tf_op jit(solution)/shard_map/transpose | solution.py:136
  76.7 4.9 %all-to-all-start.3 = ((bf16[4,320,640]{2,1,0:T(8,128)(2,1)}), bf16[4,320,640]{2,1,0:T(8,128)(2,1)}, u32[]{:S(2)}, u32[]{:S(2)}) async-start(bf16[4,320,640]{2,1,0:T(8,128)(2,1)} %bitcast.71), calls=%async_computation.3 | async-start | bytes 3276800 | tf_op jit(solution)/shard_map/all_to_all | solution.py:135
  81.6 19.9 %collective-permute-done.53.refs_4_ = bf16[48,5120]{1,0:T(8,128)(2,1)S(1)} collective-permute-done((bf16[48,5120]{1,0:T(8,128)(2,1)}, bf16[48,5120]{1,0:T(8,128)(2,1)S(1)}, u32[]{:S(2)}, u32[]{:S(2)}) %collective-permute-start.53) | collective-permute-done | bytes 491552 | tf_op jit(solution)/shard_map/ppermute | solution.py:122
  112.1 25.5 %collective-permute-done.58.refs_3_ = bf16[48,5120]{1,0:T(8,128)(2,1)S(1)} collective-permute-done((bf16[48,5120]{1,0:T(8,128)(2,1)S(1)}, bf16[48,5120]{1,0:T(8,128)(2,1)S(1)}, u32[]{:S(2)}, u32[]{:S(2)}) %collective-permute-start.58) | collective-permute-done | bytes 491552 | tf_op jit(solution)/shard_map/ppermute | solution.py:122
  145.9 9.6 %first_scores.6 = (f32[2,128,128]{2,1,0:T(8,128)S(1)}, f32[320,1536]{1,0:T(8,128)}, bf16[4,1536,640]{2,1,0:T(8,128)(2,1)}, bf16[4,1536,640]{2,1,0:T(8,128)(2,1)}) custom-call(s32[8]{0:T(128)S(1)} %stack.160.offsets_ref, bf16[384,5120]{1,0:T(8,128)(2,1)} %fusion.15.refs_0_, bf16[96,5120]{1,0:T(8,128)(2,1)} %copy-done.12, bf16[96,5120]{1,0:T(8,128)(2,1)} %copy-done.6, ...), custom_call_target="tpu_custom_call" | custom-call | flops 2516582400 | bytes 15728640 | tf_op jit(solution)/shard_map/first_scores/pallas_call | solution.py:224
  155.5 2.4 collective-permute-done.64.refs_9_
  158.0 9.2 %first_scores.7 = (f32[2,128,128]{2,1,0:T(8,128)S(1)}, f32[320,1536]{1,0:T(8,128)}, bf16[4,1536,640]{2,1,0:T(8,128)(2,1)}, bf16[4,1536,640]{2,1,0:T(8,128)(2,1)}) custom-call(s32[8]{0:T(128)S(1)} %stack.160.offsets_ref, bf16[96,5120]{1,0:T(8,128)(2,1)} %copy-done.2, ...), custom_call_target="tpu_custom_call", output_to_operand_aliasing={{1}: (16, {}), {2}: (17, {}), {3}: (18, {})} | custom-call | flops 2516582400 | bytes 15728640 | tf_op jit(solution)/shard_map/first_scores/pallas_call | solution.py:224
  167.4 79.3 %conditional.3 = (f32[16,8]{0,1:T(8,128)}, f32[640,1280]{1,0:T(8,128)}) conditional(s32[]{:T(128)} %convert_element_type.116, (f32[8,16]{1,0:T(8,128)S(1)}, s32[]{:T(128)}, pred[8]{0:T(512)(128)(4,1)S(1)}, f32[4,1,384]{2,1,0:T(1,128)S(1)}, f32[4,128,1]{1,0,2:T(4,128)S(1)}, /*index=5*/f32[4,128,1]{1,0,2:T(4,128)S(1)}, ...), branch_computations={%region_23.33_spmd, %region_33.49_spmd} | conditional | flops 15953286144 | bytes 220147200
  175.4 2.5 %collective-permute-start.5 = (f32[8,128]{1,0:T(8,128)S(1)}, f32[8,128]{1,0:T(8,128)S(1)}, u32[]{:S(2)}, u32[]{:S(2)}) collective-permute-start(f32[8,128]{1,0:T(8,128)S(1)} %add_add_fusion.1), channel_id=1, source_target_pairs={{0,6},{1,7},{2,4},{3,5},{4,2},{5,3},{6,0},{7,1},{8,14},{9,15},{10,... | collective-permute-start | bytes 12296 | tf_op jit(solution)/shard_map/cond/branch_0_fun/ppermute | solution.py:92
  178.1 2.7 %collective-permute-done.5 = f32[8,128]{1,0:T(8,128)S(1)} collective-permute-done((f32[8,128]{1,0:T(8,128)S(1)}, f32[8,128]{1,0:T(8,128)S(1)}, u32[]{:S(2)}, u32[]{:S(2)}) %collective-permute-start.5) | collective-permute-done | bytes 4128 | tf_op jit(solution)/shard_map/cond/branch_0_fun/ppermute | solution.py:92
  183.7 2.6 %collective-permute-done.6.refs_3_ = bf16[320,1536]{1,0:T(8,128)(2,1)S(1)} collective-permute-done((bf16[320,1536]{1,0:T(8,128)(2,1)S(1)}, bf16[320,1536]{1,0:T(8,128)(2,1)S(1)}, u32[]{:S(2)}, u32[]{:S(2)}) %collective-permute-start.6) | collective-permute-done | bytes 983072 | tf_op jit(solution)/shard_map/cond/branch_0_fun/ppermute | solution.py:97
  186.3 11.0 %grads_and_fresh.2 = (bf16[4,320,640]{2,1,0:T(8,128)(2,1)}, bf16[4,320,640]{2,1,0:T(8,128)(2,1)}) custom-call(bf16[4,320,640]{2,1,0:T(8,128)(2,1)} %get-tuple-element.109.refs_0_, bf16[320,1536]{1,0:T(8,128)(2,1)S(1)} %multiply_convert_fusion.refs_1_, bf16[4,1536,640]{2,1,0:T(8,128)(2,1)} %get-tuple-element.107.refs_2_.kept_ref, ...), custom_call_target="tpu_custom_call" | custom-call | flops 5033164800 | bytes 15728640 | tf_op jit(solution)/shard_map/cond/branch_0_fun/grads_and_fresh/pallas_call | solution.py:326
  197.4 4.4 %all-to-all-start = ((bf16[4,320,640]{2,1,0:T(8,128)(2,1)}), bf16[4,320,640]{2,1,0:T(8,128)(2,1)}, u32[]{:S(2)}, u32[]{:S(2)}) async-start(bf16[4,320,640]{2,1,0:T(8,128)(2,1)} %get-tuple-element.123), calls=%async_computation | async-start | bytes 3276800 | tf_op jit(solution)/shard_map/cond/branch_0_fun/all_to_all | solution.py:431
  203.3 13.2 %fresh_scores.3 = f32[4,128,128]{2,1,0:T(8,128)S(1)} custom-call(bf16[4,1536,640]{2,1,0:T(8,128)(2,1)} %get-tuple-element.107.refs_2_.kept_ref, bf16[4,1536,640]{2,1,0:T(8,128)(2,1)} %get-tuple-element.108.given_ref, bf16[4,320,640]{2,1,0:T(8,128)(2,1)} %get-tuple-element.121.own_w, bf16[4,320,640]{2,1,0:T(8,128)(2,1)} %copy-done.8, ...), custom_call_target="tpu_custom_call" | custom-call | flops 5033164800 | bytes 15728640 | tf_op jit(solution)/shard_map/cond/branch_0_fun/fresh_scores/pallas_call | solution.py:281
  222.6 2.6 %collective-permute-done.11 = f32[8,128]{1,0:T(8,128)S(1)} collective-permute-done((f32[8,128]{1,0:T(8,128)S(1)}, f32[8,128]{1,0:T(8,128)S(1)}, u32[]{:S(2)}, u32[]{:S(2)}) %collective-permute-start.11) | collective-permute-done | bytes 4128 | tf_op jit(solution)/shard_map/cond/branch_0_fun/ppermute | solution.py:102
  229.3 4.5 %collective-permute-start.13 = (f32[8,128]{1,0:T(8,128)S(1)}, f32[8,128]{1,0:T(8,128)S(1)}, u32[]{:S(2)}, u32[]{:S(2)}) collective-permute-start(f32[8,128]{1,0:T(8,128)S(1)} %add.279), channel_id=1, source_target_pairs={{0,4},{1,5},{2,6},{3,7},{4,0},{5,1},{6,2},{7,3},{8,12},{9,13},{10,... | collective-permute-start | bytes 12296 | tf_op jit(solution)/shard_map/cond/branch_0_fun/ppermute | solution.py:102
  233.9 7.3 %collective-permute-done.13 = f32[8,128]{1,0:T(8,128)S(1)} collective-permute-done((f32[8,128]{1,0:T(8,128)S(1)}, f32[8,128]{1,0:T(8,128)S(1)}, u32[]{:S(2)}, u32[]{:S(2)}) %collective-permute-start.13) | collective-permute-done | bytes 4128 | tf_op jit(solution)/shard_map/cond/branch_0_fun/ppermute | solution.py:102
  243.8 3.0 %copy.78 = f32[640,1280]{1,0:T(8,128)} copy(f32[640,1280]{0,1:T(8,128)S(1)} %convert_bitcast_fusion) | data formatting | bytes 6553600 | tf_op jit(solution)/shard_map/conditional.1
  (176 shorter events, 65.9 us)
Async XLA Ops:
  7.0 24.8 %collective-permute-start.47 = (bf16[96,5120]{1,0:T(8,128)(2,1)S(1)}, bf16[96,5120]{1,0:T(8,128)(2,1)S(1)}, u32[]{:S(2)}, u32[]{:S(2)}) collective-permute-start(bf16[96,5120]{1,0:T(8,128)(2,1)S(1)} %multiply_convert_fusion.5), channel_id=1, source_target_pairs={{0,2},{1,3},{2,0},{3,1},{4,6},{5,7},{6,4},{7,5},{8,10},{9,11},{10,... | collective-permute-start | bytes 2949128 | tf_op jit(solution)/shard_map/ppermute | solution.py:116
  10.0 21.8 %collective-permute-start.48 = (bf16[96,5120]{1,0:T(8,128)(2,1)S(1)}, bf16[96,5120]{1,0:T(8,128)(2,1)}, u32[]{:S(2)}, u32[]{:S(2)}) collective-permute-start(bf16[96,5120]{1,0:T(8,128)(2,1)S(1)} %multiply_convert_fusion.5), channel_id=1, source_target_pairs={{2,4},{3,5},{4,2},{5,3},{10,12},{11,13},{12,10},{13,11},{18,20},{1... | collective-permute-start | bytes 2949128 | tf_op jit(solution)/shard_map/ppermute | solution.py:116
  31.8 33.0 %collective-permute-start.49 = (bf16[96,5120]{1,0:T(8,128)(2,1)S(1)}, bf16[96,5120]{1,0:T(8,128)(2,1)S(1)}, u32[]{:S(2)}, u32[]{:S(2)}) collective-permute-start(bf16[96,5120]{1,0:T(8,128)(2,1)S(1)} %collective-permute-done.47.refs_1_), channel_id=1, source_target_pairs={{0,8},{8,0},{16,24},{24,16},{1,9},{9,1},{17,25},{25,17},{2,10},{10... | collective-permute-start | bytes 2949128 | tf_op jit(solution)/shard_map/ppermute | solution.py:119
  33.5 31.3 %collective-permute-start.50 = (bf16[96,5120]{1,0:T(8,128)(2,1)S(1)}, bf16[96,5120]{1,0:T(8,128)(2,1)S(1)}, u32[]{:S(2)}, u32[]{:S(2)}) collective-permute-start(bf16[96,5120]{1,0:T(8,128)(2,1)S(1)} %collective-permute-done.47.refs_1_), channel_id=1, source_target_pairs={{0,16},{8,24},{16,0},{24,8},{1,17},{9,25},{17,1},{25,9},{2,18},{10... | collective-permute-start | bytes 2949128 | tf_op jit(solution)/shard_map/ppermute | solution.py:122
  35.0 29.8 %collective-permute-start.52 = (bf16[96,5120]{1,0:T(8,128)(2,1)S(1)}, bf16[96,5120]{1,0:T(8,128)(2,1)}, u32[]{:S(2)}, u32[]{:S(2)}) collective-permute-start(bf16[96,5120]{1,0:T(8,128)(2,1)S(1)} %collective-permute-done.47.refs_1_), channel_id=1, source_target_pairs={{2,4},{3,5},{4,2},{5,3},{10,12},{11,13},{12,10},{13,11},{18,20},{1... | collective-permute-start | bytes 2949128 | tf_op jit(solution)/shard_map/ppermute | solution.py:116
  36.7 28.2 %collective-permute-start.51 = (bf16[96,5120]{1,0:T(8,128)(2,1)}, bf16[96,5120]{1,0:T(8,128)(2,1)}, u32[]{:S(2)}, u32[]{:S(2)}) collective-permute-start(bf16[96,5120]{1,0:T(8,128)(2,1)} %collective-permute-done.48), channel_id=1, source_target_pairs={{2,0},{3,1},{4,6},{5,7},{10,8},{11,9},{12,14},{13,15},{18,16},{19,... | collective-permute-start | bytes 2949128 | tf_op jit(solution)/shard_map/ppermute | solution.py:116
  39.2 25.5 %all-to-all-start.2 = ((f32[8,1,384]{2,1,0:T(1,128)}), f32[8,1,384]{2,1,0:T(1,128)S(1)}, u32[]{:S(2)}, u32[]{:S(2)}) async-start(f32[8,1,384]{2,1,0:T(1,128)} %broadcast_in_dim.585), calls=%async_computation.2 | async-start | bytes 24576 | tf_op jit(solution)/shard_map/all_to_all | solution.py:108
  66.8 34.6 %collective-permute-start.55 = (bf16[96,5120]{1,0:T(8,128)(2,1)S(1)}, bf16[96,5120]{1,0:T(8,128)(2,1)}, u32[]{:S(2)}, u32[]{:S(2)}) collective-permute-start(bf16[96,5120]{1,0:T(8,128)(2,1)S(1)} %broadcast_select_fusion.3.refs_0_), channel_id=1, source_target_pairs={{0,8},{8,0},{16,24},{24,16},{1,9},{9,1},{17,25},{25,17},{2,10},{10... | collective-permute-start | bytes 2949128 | tf_op jit(solution)/shard_map/ppermute | solution.py:119
  67.5 34.0 %collective-permute-start.56 = (bf16[96,5120]{1,0:T(8,128)(2,1)S(1)}, bf16[96,5120]{1,0:T(8,128)(2,1)}, u32[]{:S(2)}, u32[]{:S(2)}) collective-permute-start(bf16[96,5120]{1,0:T(8,128)(2,1)S(1)} %broadcast_select_fusion.3.refs_0_), channel_id=1, source_target_pairs={{0,16},{8,24},{16,0},{24,8},{1,17},{9,25},{17,1},{25,9},{2,18},{10... | collective-permute-start | bytes 2949128 | tf_op jit(solution)/shard_map/ppermute | solution.py:122
  68.0 35.7 %collective-permute-start.57 = (bf16[96,5120]{1,0:T(8,128)(2,1)}, bf16[96,5120]{1,0:T(8,128)(2,1)}, u32[]{:S(2)}, u32[]{:S(2)}) collective-permute-start(bf16[96,5120]{1,0:T(8,128)(2,1)} %collective-permute-done.52), channel_id=1, source_target_pairs={{2,0},{3,1},{4,6},{5,7},{10,8},{11,9},{12,14},{13,15},{18,16},{19,... | collective-permute-start | bytes 2949128 | tf_op jit(solution)/shard_map/ppermute | solution.py:116
  70.1 31.4 %collective-permute-start.53 = (bf16[48,5120]{1,0:T(8,128)(2,1)}, bf16[48,5120]{1,0:T(8,128)(2,1)S(1)}, u32[]{:S(2)}, u32[]{:S(2)}) collective-permute-start(bf16[48,5120]{1,0:T(8,128)(2,1)} %slice.293), channel_id=1, source_target_pairs={{0,16},{8,24},{16,0},{24,8},{1,17},{9,25},{17,1},{25,9},{2,18},{10... | collective-permute-start | bytes 1474568 | tf_op jit(solution)/shard_map/ppermute | solution.py:122
  71.6 29.8 %collective-permute-start.54 = (bf16[48,5120]{1,0:T(8,128)(2,1)S(1)}, bf16[48,5120]{1,0:T(8,128)(2,1)S(1)}, u32[]{:S(2)}, u32[]{:S(2)}) collective-permute-start(bf16[48,5120]{1,0:T(8,128)(2,1)S(1)} %slice.294), channel_id=1, source_target_pairs={{0,8},{8,0},{16,24},{24,16},{1,9},{9,1},{17,25},{25,17},{2,10},{10... | collective-permute-start | bytes 1474568 | tf_op jit(solution)/shard_map/ppermute | solution.py:119
  76.7 60.9 %all-to-all-start.3 = ((bf16[4,320,640]{2,1,0:T(8,128)(2,1)}), bf16[4,320,640]{2,1,0:T(8,128)(2,1)}, u32[]{:S(2)}, u32[]{:S(2)}) async-start(bf16[4,320,640]{2,1,0:T(8,128)(2,1)} %bitcast.71), calls=%async_computation.3 | async-start | bytes 3276800 | tf_op jit(solution)/shard_map/all_to_all | solution.py:135
  104.9 32.6 %collective-permute-start.60 = (bf16[96,5120]{1,0:T(8,128)(2,1)S(1)}, bf16[96,5120]{1,0:T(8,128)(2,1)}, u32[]{:S(2)}, u32[]{:S(2)}) collective-permute-start(bf16[96,5120]{1,0:T(8,128)(2,1)S(1)} %broadcast_select_fusion.2.refs_5_), channel_id=1, source_target_pairs={{0,8},{8,0},{16,24},{24,16},{1,9},{9,1},{17,25},{25,17},{2,10},{10... | collective-permute-start | bytes 2949128 | tf_op jit(solution)/shard_map/ppermute | solution.py:119
  106.7 30.9 %collective-permute-start.61 = (bf16[96,5120]{1,0:T(8,128)(2,1)S(1)}, bf16[96,5120]{1,0:T(8,128)(2,1)}, u32[]{:S(2)}, u32[]{:S(2)}) collective-permute-start(bf16[96,5120]{1,0:T(8,128)(2,1)S(1)} %broadcast_select_fusion.2.refs_5_), channel_id=1, source_target_pairs={{0,16},{8,24},{16,0},{24,8},{1,17},{9,25},{17,1},{25,9},{2,18},{10... | collective-permute-start | bytes 2949128 | tf_op jit(solution)/shard_map/ppermute | solution.py:122
  109.4 28.2 %collective-permute-start.58 = (bf16[48,5120]{1,0:T(8,128)(2,1)S(1)}, bf16[48,5120]{1,0:T(8,128)(2,1)S(1)}, u32[]{:S(2)}, u32[]{:S(2)}) collective-permute-start(bf16[48,5120]{1,0:T(8,128)(2,1)S(1)} %slice.295), channel_id=1, source_target_pairs={{0,16},{8,24},{16,0},{24,8},{1,17},{9,25},{17,1},{25,9},{2,18},{10... | collective-permute-start | bytes 1474568 | tf_op jit(solution)/shard_map/ppermute | solution.py:122
  111.7 25.9 %collective-permute-start.59 = (bf16[48,5120]{1,0:T(8,128)(2,1)}, bf16[48,5120]{1,0:T(8,128)(2,1)S(1)}, u32[]{:S(2)}, u32[]{:S(2)}) collective-permute-start(bf16[48,5120]{1,0:T(8,128)(2,1)} %slice.296), channel_id=1, source_target_pairs={{0,8},{8,0},{16,24},{24,16},{1,9},{9,1},{17,25},{25,17},{2,10},{10... | collective-permute-start | bytes 1474568 | tf_op jit(solution)/shard_map/ppermute | solution.py:119
  137.6 8.3 %collective-permute-start.62 = (bf16[4,320,640]{2,1,0:T(8,128)(2,1)}, bf16[4,320,640]{2,1,0:T(8,128)(2,1)}, u32[]{:S(2)}, u32[]{:S(2)}) collective-permute-start(bf16[4,320,640]{2,1,0:T(8,128)(2,1)} %all-to-all-done.3.refs_6_.refs_10_), channel_id=1, source_target_pairs={{0,1},{1,0},{2,3},{3,2},{4,5},{5,4},{6,7},{7,6},{8,9},{9,8},{10,11... | collective-permute-start | bytes 4915208 | tf_op jit(solution)/shard_map/ppermute | solution.py:97
  141.0 14.6 %collective-permute-start.63 = (bf16[48,5120]{1,0:T(8,128)(2,1)S(1)}, bf16[48,5120]{1,0:T(8,128)(2,1)S(1)}, u32[]{:S(2)}, u32[]{:S(2)}) collective-permute-start(bf16[48,5120]{1,0:T(8,128)(2,1)S(1)} %slice.299), channel_id=1, source_target_pairs={{0,16},{8,24},{16,0},{24,8},{1,17},{9,25},{17,1},{25,9},{2,18},{10... | collective-permute-start | bytes 1474568 | tf_op jit(solution)/shard_map/ppermute | solution.py:122
  144.4 13.6 %collective-permute-start.64 = (bf16[48,5120]{1,0:T(8,128)(2,1)}, bf16[48,5120]{1,0:T(8,128)(2,1)}, u32[]{:S(2)}, u32[]{:S(2)}) collective-permute-start(bf16[48,5120]{1,0:T(8,128)(2,1)} %slice.300), channel_id=1, source_target_pairs={{0,8},{8,0},{16,24},{24,16},{1,9},{9,1},{17,25},{25,17},{2,10},{10... | collective-permute-start | bytes 1474568 | tf_op jit(solution)/shard_map/ppermute | solution.py:119
  167.5 18.8 %collective-permute-start.7 = (bf16[4,1536,640]{2,1,0:T(8,128)(2,1)}, bf16[4,1536,640]{2,1,0:T(8,128)(2,1)}, u32[]{:S(2)}, u32[]{:S(2)}) collective-permute-start(bf16[4,1536,640]{2,1,0:T(8,128)(2,1)} %get-tuple-element.108.given_ref), channel_id=1, source_target_pairs={{0,1},{1,0},{2,3},{3,2},{4,5},{5,4},{6,7},{7,6},{8,9},{9,8},{10,11... | collective-permute-start | bytes 23592968 | tf_op jit(solution)/shard_map/cond/branch_0_fun/ppermute | solution.py:97
  175.4 5.4 %collective-permute-start.5 = (f32[8,128]{1,0:T(8,128)S(1)}, f32[8,128]{1,0:T(8,128)S(1)}, u32[]{:S(2)}, u32[]{:S(2)}) collective-permute-start(f32[8,128]{1,0:T(8,128)S(1)} %add_add_fusion.1), channel_id=1, source_target_pairs={{0,6},{1,7},{2,4},{3,5},{4,2},{5,3},{6,0},{7,1},{8,14},{9,15},{10,... | collective-permute-start | bytes 12296 | tf_op jit(solution)/shard_map/cond/branch_0_fun/ppermute | solution.py:92
  197.4 44.7 %all-to-all-start = ((bf16[4,320,640]{2,1,0:T(8,128)(2,1)}), bf16[4,320,640]{2,1,0:T(8,128)(2,1)}, u32[]{:S(2)}, u32[]{:S(2)}) async-start(bf16[4,320,640]{2,1,0:T(8,128)(2,1)} %get-tuple-element.123), calls=%async_computation | async-start | bytes 3276800 | tf_op jit(solution)/shard_map/cond/branch_0_fun/all_to_all | solution.py:431
  229.3 11.9 %collective-permute-start.13 = (f32[8,128]{1,0:T(8,128)S(1)}, f32[8,128]{1,0:T(8,128)S(1)}, u32[]{:S(2)}, u32[]{:S(2)}) collective-permute-start(f32[8,128]{1,0:T(8,128)S(1)} %add.279), channel_id=1, source_target_pairs={{0,4},{1,5},{2,6},{3,7},{4,0},{5,1},{6,2},{7,3},{8,12},{9,13},{10,... | collective-permute-start | bytes 12296 | tf_op jit(solution)/shard_map/cond/branch_0_fun/ppermute | solution.py:102
  (26 other events, 275.8 us)

commit v3 on v2

--- a/solution.py
+++ b/solution.py
@@ -173,36 +173,44 @@
     wide = own_w.shape[2]
     tile, width = x_s.shape
     depth = width // blocks
-    copies = []
-    at = 0
-    for index, size in enumerate(sizes):
-        copies.append(pltpu.make_async_copy(parts[index], x_s.at[pl.ds(at, size)], in_sem.at[index]))
-        at += size
-    for core, source in enumerate((own_w, mate_w)):
-        for j in range(4):
+    loads = []
+    for j in range(blocks):
+        columns = pl.ds(j * depth, depth)
+        here = []
+        for core, source in enumerate((own_w, mate_w)):
             where = pl.ds(pl.multiple_of(offsets_ref[core * 4 + j], 128), wide)
-            copies.append(pltpu.make_async_copy(source.at[j], w_s.at[:, where], w_sem.at[core * 4 + j]))
-    for copy in copies:
-        copy.start()
-    acc_s[...] = jnp.zeros_like(acc_s)
-    for copy in copies:
-        copy.wait()
+            here.append(pltpu.make_async_copy(source.at[j], w_s.at[:, where], w_sem.at[core * 4 + j]))
+        at = 0
+        for index, size in enumerate(sizes):
+            here.append(
+                pltpu.make_async_copy(
+                    parts[index].at[:, columns], x_s.at[pl.ds(at, size), columns], in_sem.at[j, index]
+                )
+            )
+            at += size
+        loads.append(here)
+    for here in loads:
+        for copy in here:
+            copy.start()
     rows = pl.ds(first, tile)
     out_copies = []
-    for core, dest in enumerate((kept_ref, given_ref)):
-        for j in range(4):
+    for j in range(blocks):
+        for copy in loads[j]:
+            copy.wait()
+        for core, dest in enumerate((kept_ref, given_ref)):
             where = pl.ds(pl.multiple_of(offsets_ref[core * 4 + j], 128), wide)
             out_copies.append(
                 pltpu.make_async_copy(x_s.at[:, where], dest.at[j, rows], out_sem.at[core * 4 + j])
             )
             out_copies[-1].start()
-
-    @pl.loop(0, blocks)
-    def _(k):
-        where = pl.ds(pl.multiple_of(k * depth, 128), depth)
-        acc_s[...] += lax.dot_general(
-            w_s[:, where], x_s[:, where], (((1,), (1,)), ((), ())), preferred_element_type=jnp.float32
+        columns = pl.ds(j * depth, depth)
+        term = lax.dot_general(
+            w_s[:, columns], x_s[:, columns], (((1,), (1,)), ((), ())), preferred_element_type=jnp.float32
         )
+        if j == 0:
+            acc_s[...] = term
+        else:
+            acc_s[...] += term
 
     out_copies.append(pltpu.make_async_copy(acc_s, pre_ref.at[:, rows], out_sem.at[8]))
     out_copies[-1].start()
@@ -222,7 +230,7 @@
     total = tile // chips * 4
     first_carried = 1 + len(parts) + 5
     return pl.pallas_call(
-        functools.partial(first_kernel, sizes=sizes, blocks=5, first=first * (tile // chips), carried=len(carried)),
+        functools.partial(first_kernel, sizes=sizes, blocks=4, first=first * (tile // chips), carried=len(carried)),
         out_shape=(
             jax.ShapeDtypeStruct((chips, bounds.shape[1], 128), jnp.float32),
             jax.ShapeDtypeStruct((units, total), jnp.float32),
@@ -239,7 +247,7 @@
             pltpu.VMEM((tile, width), jnp.bfloat16),
             pltpu.VMEM((units, width), jnp.bfloat16),
             pltpu.VMEM((units, tile), jnp.float32),
-            pltpu.SemaphoreType.DMA((len(parts),)),
+            pltpu.SemaphoreType.DMA((4, len(parts))),
             pltpu.SemaphoreType.DMA((8,)),
             pltpu.SemaphoreType.DMA((9,)),
         ],

time: 248 us -> 248 us (level)
  no operation moved by 1% of the time
where the time goes in v3:
time: 248 us; the launch traced here: 247 us
  waiting for transfers between devices  103 us (42%)
  starting transfers between devices  58.3 us (24%)
  Pallas kernels  43.3 us (17%)
  local copies, waits for them, and re-layouts  18.2 us (7%)
  other arithmetic  15.5 us (6%)
  matrix products  6.16 us (2%)
    ppermute x6, waiting for transfers between devices, y_of(): return lax.ppermute(values, 'rep', Y_MATE)  45.4 us
    pallas_call x2, Pallas kernels, first_scores(): pl.pallas_call(functools.partial(first_kernel, sizes=sizes, blocks=4, fir...  19.2 us
    all_to_all x1, waiting for transfers between devices, gather_small(): lax.all_to_all(copies, 'fsdp', split_axis=0, concat_axis=0, tiled=True)  16.7 us
    ppermute x5, waiting for transfers between devices, along(): return lax.ppermute(values, 'fsdp', pairs)  16.6 us
    ppermute x4, waiting for transfers between devices, sum_in_turn(): values = values + lax.ppermute(values, axis, pairs)  14.1 us
    pallas_call x1, Pallas kernels, fresh_scores(): pl.pallas_call(fresh_kernel, grid=(2, 4), out_shape=jax.ShapeDtypeStruct(...  13.2 us
    pallas_call x1, Pallas kernels, grads_and_fresh(): pl.pallas_call(functools.partial(grad_kernel, rate, len(terms)), grid=(4,...  11 us
    ppermute x5, starting transfers between devices, along(): return lax.ppermute(values, 'fsdp', pairs)  8.97 us
  transfers between devices with their start and end apart: 35, of which 17 were waited for; matrix products, arithmetic and copies ran while one was open for 10% of the time, Pallas kernels for 9%

profile of v3, /device:TPU:0, one launch (start us, length us, event | category | flops | bytes accessed | tf_op | source)
XLA Modules:
  0.0 246.8 jit_solution(7239603165616286454)
XLA Ops:
  2.9 3.8 %multiply_reduce_fusion.2 = (f32[96]{0:T(128)S(1)}, f32[96,5120]{1,0:T(8,128)S(1)}) fusion(bf16[512,5120]{1,0:T(8,128)(2,1)} %bitcast.130, s32[512]{0:T(512)S(1)} %select_n.236, s32[96]{0:T(128)S(1)} %get-tuple-element.582), kind=kOutput, calls=%fused_computation.139 | convolution fusion | flops 505331616 | bytes 7211776 | tf_op jit(solution)/shard_map/dot_general | solution.py:369
  7.0 3.1 %collective-permute-start.47 = (bf16[96,5120]{1,0:T(8,128)(2,1)S(1)}, bf16[96,5120]{1,0:T(8,128)(2,1)S(1)}, u32[]{:S(2)}, u32[]{:S(2)}) collective-permute-start(bf16[96,5120]{1,0:T(8,128)(2,1)S(1)} %multiply_convert_fusion.5), channel_id=1, source_target_pairs={{0,2},{1,3},{2,0},{3,1},{4,6},{5,7},{6,4},{7,5},{8,10},{9,11},{10,... | collective-permute-start | bytes 2949128 | tf_op jit(solution)/shard_map/ppermute | solution.py:116
  14.1 3.2 %fusion.15.refs_0_ = bf16[384,5120]{1,0:T(8,128)(2,1)} fusion(bf16[384,5120]{1,0:T(8,128)(2,1)S(1)} %get-tuple-element.576, f32[5120]{0:T(1024)S(1)} %copy-done.17, f32[384]{0:T(512)S(1)} %add_rsqrt_fusion.2), kind=kLoop, calls=%fused_computation.134 | loop fusion | flops 7864320 | bytes 7886336 | tf_op jit(solution)/shard_map/convert_element_type | solution.py:25
  17.3 14.5 %collective-permute-done.47.refs_1_ = bf16[96,5120]{1,0:T(8,128)(2,1)S(1)} collective-permute-done((bf16[96,5120]{1,0:T(8,128)(2,1)S(1)}, bf16[96,5120]{1,0:T(8,128)(2,1)S(1)}, u32[]{:S(2)}, u32[]{:S(2)}) %collective-permute-start.47) | collective-permute-done | bytes 983072 | tf_op jit(solution)/shard_map/ppermute | solution.py:116
  39.2 8.9 %all-to-all-start.2 = ((f32[8,1,384]{2,1,0:T(1,128)}), f32[8,1,384]{2,1,0:T(1,128)S(1)}, u32[]{:S(2)}, u32[]{:S(2)}) async-start(f32[8,1,384]{2,1,0:T(1,128)} %broadcast_in_dim.585), calls=%async_computation.2 | async-start | bytes 24576 | tf_op jit(solution)/shard_map/all_to_all | solution.py:108
  48.1 16.7 %all-to-all-done.2 = f32[8,1,384]{2,1,0:T(1,128)S(1)} async-done(((f32[8,1,384]{2,1,0:T(1,128)}), f32[8,1,384]{2,1,0:T(1,128)S(1)}, u32[]{:S(2)}, u32[]{:S(2)}) %all-to-all-start.2) | async-done | bytes 12320 | tf_op jit(solution)/shard_map/all_to_all | solution.py:108
  73.2 3.5 %copy.60 = bf16[1280,640]{1,0:T(8,128)(2,1)} copy(bf16[1280,640]{0,1:T(8,128)(2,1)} %bitcast.135) | data formatting | bytes 3276800 | tf_op jit(solution)/shard_map/transpose | solution.py:136
  76.7 4.9 %all-to-all-start.3 = ((bf16[4,320,640]{2,1,0:T(8,128)(2,1)}), bf16[4,320,640]{2,1,0:T(8,128)(2,1)}, u32[]{:S(2)}, u32[]{:S(2)}) async-start(bf16[4,320,640]{2,1,0:T(8,128)(2,1)} %bitcast.71), calls=%async_computation.3 | async-start | bytes 3276800 | tf_op jit(solution)/shard_map/all_to_all | solution.py:135
  81.6 19.9 %collective-permute-done.53.refs_4_ = bf16[48,5120]{1,0:T(8,128)(2,1)S(1)} collective-permute-done((bf16[48,5120]{1,0:T(8,128)(2,1)}, bf16[48,5120]{1,0:T(8,128)(2,1)S(1)}, u32[]{:S(2)}, u32[]{:S(2)}) %collective-permute-start.53) | collective-permute-done | bytes 491552 | tf_op jit(solution)/shard_map/ppermute | solution.py:122
  112.1 25.5 %collective-permute-done.58.refs_3_ = bf16[48,5120]{1,0:T(8,128)(2,1)S(1)} collective-permute-done((bf16[48,5120]{1,0:T(8,128)(2,1)S(1)}, bf16[48,5120]{1,0:T(8,128)(2,1)S(1)}, u32[]{:S(2)}, u32[]{:S(2)}) %collective-permute-start.58) | collective-permute-done | bytes 491552 | tf_op jit(solution)/shard_map/ppermute | solution.py:122
  145.9 9.7 %first_scores.6 = (f32[2,128,128]{2,1,0:T(8,128)S(1)}, f32[320,1536]{1,0:T(8,128)}, bf16[4,1536,640]{2,1,0:T(8,128)(2,1)}, bf16[4,1536,640]{2,1,0:T(8,128)(2,1)}) custom-call(s32[8]{0:T(128)S(1)} %stack.160.offsets_ref, bf16[384,5120]{1,0:T(8,128)(2,1)} %fusion.15.refs_0_, bf16[96,5120]{1,0:T(8,128)(2,1)} %copy-done.12, bf16[96,5120]{1,0:T(8,128)(2,1)} %copy-done.6, ...), custom_call_target="tpu_custom_call" | custom-call | flops 2516582400 | bytes 15728640 | tf_op jit(solution)/shard_map/first_scores/pallas_call | solution.py:232
  158.0 9.5 %first_scores.7 = (f32[2,128,128]{2,1,0:T(8,128)S(1)}, f32[320,1536]{1,0:T(8,128)}, bf16[4,1536,640]{2,1,0:T(8,128)(2,1)}, bf16[4,1536,640]{2,1,0:T(8,128)(2,1)}) custom-call(s32[8]{0:T(128)S(1)} %stack.160.offsets_ref, bf16[96,5120]{1,0:T(8,128)(2,1)} %copy-done.2, ...), custom_call_target="tpu_custom_call", output_to_operand_aliasing={{1}: (16, {}), {2}: (17, {}), {3}: (18, {})} | custom-call | flops 2516582400 | bytes 15728640 | tf_op jit(solution)/shard_map/first_scores/pallas_call | solution.py:232
  167.7 79.2 %conditional.3 = (f32[16,8]{0,1:T(8,128)}, f32[640,1280]{1,0:T(8,128)}) conditional(s32[]{:T(128)} %convert_element_type.116, (f32[8,16]{1,0:T(8,128)S(1)}, s32[]{:T(128)}, pred[8]{0:T(512)(128)(4,1)S(1)}, f32[4,1,384]{2,1,0:T(1,128)S(1)}, f32[4,128,1]{1,0,2:T(4,128)S(1)}, /*index=5*/f32[4,128,1]{1,0,2:T(4,128)S(1)}, ...), branch_computations={%region_23.33_spmd, %region_33.49_spmd} | conditional | flops 15953286144 | bytes 220147200
  169.0 2.4 collective-permute-start.2
  175.5 2.5 %collective-permute-start.5 = (f32[8,128]{1,0:T(8,128)S(1)}, f32[8,128]{1,0:T(8,128)S(1)}, u32[]{:S(2)}, u32[]{:S(2)}) collective-permute-start(f32[8,128]{1,0:T(8,128)S(1)} %add_add_fusion.1), channel_id=1, source_target_pairs={{0,6},{1,7},{2,4},{3,5},{4,2},{5,3},{6,0},{7,1},{8,14},{9,15},{10,... | collective-permute-start | bytes 12296 | tf_op jit(solution)/shard_map/cond/branch_0_fun/ppermute | solution.py:92
  178.2 2.7 %collective-permute-done.5 = f32[8,128]{1,0:T(8,128)S(1)} collective-permute-done((f32[8,128]{1,0:T(8,128)S(1)}, f32[8,128]{1,0:T(8,128)S(1)}, u32[]{:S(2)}, u32[]{:S(2)}) %collective-permute-start.5) | collective-permute-done | bytes 4128 | tf_op jit(solution)/shard_map/cond/branch_0_fun/ppermute | solution.py:92
  183.8 2.6 %collective-permute-done.6.refs_3_ = bf16[320,1536]{1,0:T(8,128)(2,1)S(1)} collective-permute-done((bf16[320,1536]{1,0:T(8,128)(2,1)S(1)}, bf16[320,1536]{1,0:T(8,128)(2,1)S(1)}, u32[]{:S(2)}, u32[]{:S(2)}) %collective-permute-start.6) | collective-permute-done | bytes 983072 | tf_op jit(solution)/shard_map/cond/branch_0_fun/ppermute | solution.py:97
  186.4 11.0 %grads_and_fresh.2 = (bf16[4,320,640]{2,1,0:T(8,128)(2,1)}, bf16[4,320,640]{2,1,0:T(8,128)(2,1)}) custom-call(bf16[4,320,640]{2,1,0:T(8,128)(2,1)} %get-tuple-element.109.refs_0_, bf16[320,1536]{1,0:T(8,128)(2,1)S(1)} %multiply_convert_fusion.refs_1_, bf16[4,1536,640]{2,1,0:T(8,128)(2,1)} %get-tuple-element.107.refs_2_.kept_ref, ...), custom_call_target="tpu_custom_call" | custom-call | flops 5033164800 | bytes 15728640 | tf_op jit(solution)/shard_map/cond/branch_0_fun/grads_and_fresh/pallas_call | solution.py:334
  197.5 4.4 %all-to-all-start = ((bf16[4,320,640]{2,1,0:T(8,128)(2,1)}), bf16[4,320,640]{2,1,0:T(8,128)(2,1)}, u32[]{:S(2)}, u32[]{:S(2)}) async-start(bf16[4,320,640]{2,1,0:T(8,128)(2,1)} %get-tuple-element.123), calls=%async_computation | async-start | bytes 3276800 | tf_op jit(solution)/shard_map/cond/branch_0_fun/all_to_all | solution.py:439
  203.4 13.2 %fresh_scores.3 = f32[4,128,128]{2,1,0:T(8,128)S(1)} custom-call(bf16[4,1536,640]{2,1,0:T(8,128)(2,1)} %get-tuple-element.107.refs_2_.kept_ref, bf16[4,1536,640]{2,1,0:T(8,128)(2,1)} %get-tuple-element.108.given_ref, bf16[4,320,640]{2,1,0:T(8,128)(2,1)} %get-tuple-element.121.own_w, bf16[4,320,640]{2,1,0:T(8,128)(2,1)} %copy-done.8, ...), custom_call_target="tpu_custom_call" | custom-call | flops 5033164800 | bytes 15728640 | tf_op jit(solution)/shard_map/cond/branch_0_fun/fresh_scores/pallas_call | solution.py:289
  222.7 2.6 %collective-permute-done.11 = f32[8,128]{1,0:T(8,128)S(1)} collective-permute-done((f32[8,128]{1,0:T(8,128)S(1)}, f32[8,128]{1,0:T(8,128)S(1)}, u32[]{:S(2)}, u32[]{:S(2)}) %collective-permute-start.11) | collective-permute-done | bytes 4128 | tf_op jit(solution)/shard_map/cond/branch_0_fun/ppermute | solution.py:102
  229.4 4.5 %collective-permute-start.13 = (f32[8,128]{1,0:T(8,128)S(1)}, f32[8,128]{1,0:T(8,128)S(1)}, u32[]{:S(2)}, u32[]{:S(2)}) collective-permute-start(f32[8,128]{1,0:T(8,128)S(1)} %add.279), channel_id=1, source_target_pairs={{0,4},{1,5},{2,6},{3,7},{4,0},{5,1},{6,2},{7,3},{8,12},{9,13},{10,... | collective-permute-start | bytes 12296 | tf_op jit(solution)/shard_map/cond/branch_0_fun/ppermute | solution.py:102
  234.0 7.3 %collective-permute-done.13 = f32[8,128]{1,0:T(8,128)S(1)} collective-permute-done((f32[8,128]{1,0:T(8,128)S(1)}, f32[8,128]{1,0:T(8,128)S(1)}, u32[]{:S(2)}, u32[]{:S(2)}) %collective-permute-start.13) | collective-permute-done | bytes 4128 | tf_op jit(solution)/shard_map/cond/branch_0_fun/ppermute | solution.py:102
  243.9 3.0 %copy.78 = f32[640,1280]{1,0:T(8,128)} copy(f32[640,1280]{0,1:T(8,128)S(1)} %convert_bitcast_fusion) | data formatting | bytes 6553600 | tf_op jit(solution)/shard_map/conditional.1
  (176 shorter events, 65.7 us)
Async XLA Ops:
  7.0 24.8 %collective-permute-start.47 = (bf16[96,5120]{1,0:T(8,128)(2,1)S(1)}, bf16[96,5120]{1,0:T(8,128)(2,1)S(1)}, u32[]{:S(2)}, u32[]{:S(2)}) collective-permute-start(bf16[96,5120]{1,0:T(8,128)(2,1)S(1)} %multiply_convert_fusion.5), channel_id=1, source_target_pairs={{0,2},{1,3},{2,0},{3,1},{4,6},{5,7},{6,4},{7,5},{8,10},{9,11},{10,... | collective-permute-start | bytes 2949128 | tf_op jit(solution)/shard_map/ppermute | solution.py:116
  10.0 21.8 %collective-permute-start.48 = (bf16[96,5120]{1,0:T(8,128)(2,1)S(1)}, bf16[96,5120]{1,0:T(8,128)(2,1)}, u32[]{:S(2)}, u32[]{:S(2)}) collective-permute-start(bf16[96,5120]{1,0:T(8,128)(2,1)S(1)} %multiply_convert_fusion.5), channel_id=1, source_target_pairs={{2,4},{3,5},{4,2},{5,3},{10,12},{11,13},{12,10},{13,11},{18,20},{1... | collective-permute-start | bytes 2949128 | tf_op jit(solution)/shard_map/ppermute | solution.py:116
  31.8 33.0 %collective-permute-start.49 = (bf16[96,5120]{1,0:T(8,128)(2,1)S(1)}, bf16[96,5120]{1,0:T(8,128)(2,1)S(1)}, u32[]{:S(2)}, u32[]{:S(2)}) collective-permute-start(bf16[96,5120]{1,0:T(8,128)(2,1)S(1)} %collective-permute-done.47.refs_1_), channel_id=1, source_target_pairs={{0,8},{8,0},{16,24},{24,16},{1,9},{9,1},{17,25},{25,17},{2,10},{10... | collective-permute-start | bytes 2949128 | tf_op jit(solution)/shard_map/ppermute | solution.py:119
  33.5 31.3 %collective-permute-start.50 = (bf16[96,5120]{1,0:T(8,128)(2,1)S(1)}, bf16[96,5120]{1,0:T(8,128)(2,1)S(1)}, u32[]{:S(2)}, u32[]{:S(2)}) collective-permute-start(bf16[96,5120]{1,0:T(8,128)(2,1)S(1)} %collective-permute-done.47.refs_1_), channel_id=1, source_target_pairs={{0,16},{8,24},{16,0},{24,8},{1,17},{9,25},{17,1},{25,9},{2,18},{10... | collective-permute-start | bytes 2949128 | tf_op jit(solution)/shard_map/ppermute | solution.py:122
  35.0 29.8 %collective-permute-start.52 = (bf16[96,5120]{1,0:T(8,128)(2,1)S(1)}, bf16[96,5120]{1,0:T(8,128)(2,1)}, u32[]{:S(2)}, u32[]{:S(2)}) collective-permute-start(bf16[96,5120]{1,0:T(8,128)(2,1)S(1)} %collective-permute-done.47.refs_1_), channel_id=1, source_target_pairs={{2,4},{3,5},{4,2},{5,3},{10,12},{11,13},{12,10},{13,11},{18,20},{1... | collective-permute-start | bytes 2949128 | tf_op jit(solution)/shard_map/ppermute | solution.py:116
  36.7 28.2 %collective-permute-start.51 = (bf16[96,5120]{1,0:T(8,128)(2,1)}, bf16[96,5120]{1,0:T(8,128)(2,1)}, u32[]{:S(2)}, u32[]{:S(2)}) collective-permute-start(bf16[96,5120]{1,0:T(8,128)(2,1)} %collective-permute-done.48), channel_id=1, source_target_pairs={{2,0},{3,1},{4,6},{5,7},{10,8},{11,9},{12,14},{13,15},{18,16},{19,... | collective-permute-start | bytes 2949128 | tf_op jit(solution)/shard_map/ppermute | solution.py:116
  39.2 25.5 %all-to-all-start.2 = ((f32[8,1,384]{2,1,0:T(1,128)}), f32[8,1,384]{2,1,0:T(1,128)S(1)}, u32[]{:S(2)}, u32[]{:S(2)}) async-start(f32[8,1,384]{2,1,0:T(1,128)} %broadcast_in_dim.585), calls=%async_computation.2 | async-start | bytes 24576 | tf_op jit(solution)/shard_map/all_to_all | solution.py:108
  66.8 34.6 %collective-permute-start.55 = (bf16[96,5120]{1,0:T(8,128)(2,1)S(1)}, bf16[96,5120]{1,0:T(8,128)(2,1)}, u32[]{:S(2)}, u32[]{:S(2)}) collective-permute-start(bf16[96,5120]{1,0:T(8,128)(2,1)S(1)} %broadcast_select_fusion.3.refs_0_), channel_id=1, source_target_pairs={{0,8},{8,0},{16,24},{24,16},{1,9},{9,1},{17,25},{25,17},{2,10},{10... | collective-permute-start | bytes 2949128 | tf_op jit(solution)/shard_map/ppermute | solution.py:119
  67.5 34.0 %collective-permute-start.56 = (bf16[96,5120]{1,0:T(8,128)(2,1)S(1)}, bf16[96,5120]{1,0:T(8,128)(2,1)}, u32[]{:S(2)}, u32[]{:S(2)}) collective-permute-start(bf16[96,5120]{1,0:T(8,128)(2,1)S(1)} %broadcast_select_fusion.3.refs_0_), channel_id=1, source_target_pairs={{0,16},{8,24},{16,0},{24,8},{1,17},{9,25},{17,1},{25,9},{2,18},{10... | collective-permute-start | bytes 2949128 | tf_op jit(solution)/shard_map/ppermute | solution.py:122
  68.0 35.7 %collective-permute-start.57 = (bf16[96,5120]{1,0:T(8,128)(2,1)}, bf16[96,5120]{1,0:T(8,128)(2,1)}, u32[]{:S(2)}, u32[]{:S(2)}) collective-permute-start(bf16[96,5120]{1,0:T(8,128)(2,1)} %collective-permute-done.52), channel_id=1, source_target_pairs={{2,0},{3,1},{4,6},{5,7},{10,8},{11,9},{12,14},{13,15},{18,16},{19,... | collective-permute-start | bytes 2949128 | tf_op jit(solution)/shard_map/ppermute | solution.py:116
  70.1 31.4 %collective-permute-start.53 = (bf16[48,5120]{1,0:T(8,128)(2,1)}, bf16[48,5120]{1,0:T(8,128)(2,1)S(1)}, u32[]{:S(2)}, u32[]{:S(2)}) collective-permute-start(bf16[48,5120]{1,0:T(8,128)(2,1)} %slice.293), channel_id=1, source_target_pairs={{0,16},{8,24},{16,0},{24,8},{1,17},{9,25},{17,1},{25,9},{2,18},{10... | collective-permute-start | bytes 1474568 | tf_op jit(solution)/shard_map/ppermute | solution.py:122
  71.6 29.8 %collective-permute-start.54 = (bf16[48,5120]{1,0:T(8,128)(2,1)S(1)}, bf16[48,5120]{1,0:T(8,128)(2,1)S(1)}, u32[]{:S(2)}, u32[]{:S(2)}) collective-permute-start(bf16[48,5120]{1,0:T(8,128)(2,1)S(1)} %slice.294), channel_id=1, source_target_pairs={{0,8},{8,0},{16,24},{24,16},{1,9},{9,1},{17,25},{25,17},{2,10},{10... | collective-permute-start | bytes 1474568 | tf_op jit(solution)/shard_map/ppermute | solution.py:119
  76.7 60.9 %all-to-all-start.3 = ((bf16[4,320,640]{2,1,0:T(8,128)(2,1)}), bf16[4,320,640]{2,1,0:T(8,128)(2,1)}, u32[]{:S(2)}, u32[]{:S(2)}) async-start(bf16[4,320,640]{2,1,0:T(8,128)(2,1)} %bitcast.71), calls=%async_computation.3 | async-start | bytes 3276800 | tf_op jit(solution)/shard_map/all_to_all | solution.py:135
  104.9 32.6 %collective-permute-start.60 = (bf16[96,5120]{1,0:T(8,128)(2,1)S(1)}, bf16[96,5120]{1,0:T(8,128)(2,1)}, u32[]{:S(2)}, u32[]{:S(2)}) collective-permute-start(bf16[96,5120]{1,0:T(8,128)(2,1)S(1)} %broadcast_select_fusion.2.refs_5_), channel_id=1, source_target_pairs={{0,8},{8,0},{16,24},{24,16},{1,9},{9,1},{17,25},{25,17},{2,10},{10... | collective-permute-start | bytes 2949128 | tf_op jit(solution)/shard_map/ppermute | solution.py:119
  106.5 31.1 %collective-permute-start.61 = (bf16[96,5120]{1,0:T(8,128)(2,1)S(1)}, bf16[96,5120]{1,0:T(8,128)(2,1)}, u32[]{:S(2)}, u32[]{:S(2)}) collective-permute-start(bf16[96,5120]{1,0:T(8,128)(2,1)S(1)} %broadcast_select_fusion.2.refs_5_), channel_id=1, source_target_pairs={{0,16},{8,24},{16,0},{24,8},{1,17},{9,25},{17,1},{25,9},{2,18},{10... | collective-permute-start | bytes 2949128 | tf_op jit(solution)/shard_map/ppermute | solution.py:122
  109.2 28.4 %collective-permute-start.58 = (bf16[48,5120]{1,0:T(8,128)(2,1)S(1)}, bf16[48,5120]{1,0:T(8,128)(2,1)S(1)}, u32[]{:S(2)}, u32[]{:S(2)}) collective-permute-start(bf16[48,5120]{1,0:T(8,128)(2,1)S(1)} %slice.295), channel_id=1, source_target_pairs={{0,16},{8,24},{16,0},{24,8},{1,17},{9,25},{17,1},{25,9},{2,18},{10... | collective-permute-start | bytes 1474568 | tf_op jit(solution)/shard_map/ppermute | solution.py:122
  111.5 26.1 %collective-permute-start.59 = (bf16[48,5120]{1,0:T(8,128)(2,1)}, bf16[48,5120]{1,0:T(8,128)(2,1)S(1)}, u32[]{:S(2)}, u32[]{:S(2)}) collective-permute-start(bf16[48,5120]{1,0:T(8,128)(2,1)} %slice.296), channel_id=1, source_target_pairs={{0,8},{8,0},{16,24},{24,16},{1,9},{9,1},{17,25},{25,17},{2,10},{10... | collective-permute-start | bytes 1474568 | tf_op jit(solution)/shard_map/ppermute | solution.py:119
  137.6 8.3 %collective-permute-start.62 = (bf16[4,320,640]{2,1,0:T(8,128)(2,1)}, bf16[4,320,640]{2,1,0:T(8,128)(2,1)}, u32[]{:S(2)}, u32[]{:S(2)}) collective-permute-start(bf16[4,320,640]{2,1,0:T(8,128)(2,1)} %all-to-all-done.3.refs_6_.refs_10_), channel_id=1, source_target_pairs={{0,1},{1,0},{2,3},{3,2},{4,5},{5,4},{6,7},{7,6},{8,9},{9,8},{10,11... | collective-permute-start | bytes 4915208 | tf_op jit(solution)/shard_map/ppermute | solution.py:97
  141.0 14.7 %collective-permute-start.63 = (bf16[48,5120]{1,0:T(8,128)(2,1)S(1)}, bf16[48,5120]{1,0:T(8,128)(2,1)S(1)}, u32[]{:S(2)}, u32[]{:S(2)}) collective-permute-start(bf16[48,5120]{1,0:T(8,128)(2,1)S(1)} %slice.299), channel_id=1, source_target_pairs={{0,16},{8,24},{16,0},{24,8},{1,17},{9,25},{17,1},{25,9},{2,18},{10... | collective-permute-start | bytes 1474568 | tf_op jit(solution)/shard_map/ppermute | solution.py:122
  144.4 13.6 %collective-permute-start.64 = (bf16[48,5120]{1,0:T(8,128)(2,1)}, bf16[48,5120]{1,0:T(8,128)(2,1)}, u32[]{:S(2)}, u32[]{:S(2)}) collective-permute-start(bf16[48,5120]{1,0:T(8,128)(2,1)} %slice.300), channel_id=1, source_target_pairs={{0,8},{8,0},{16,24},{24,16},{1,9},{9,1},{17,25},{25,17},{2,10},{10... | collective-permute-start | bytes 1474568 | tf_op jit(solution)/shard_map/ppermute | solution.py:119
  167.7 18.7 %collective-permute-start.7 = (bf16[4,1536,640]{2,1,0:T(8,128)(2,1)}, bf16[4,1536,640]{2,1,0:T(8,128)(2,1)}, u32[]{:S(2)}, u32[]{:S(2)}) collective-permute-start(bf16[4,1536,640]{2,1,0:T(8,128)(2,1)} %get-tuple-element.108.given_ref), channel_id=1, source_target_pairs={{0,1},{1,0},{2,3},{3,2},{4,5},{5,4},{6,7},{7,6},{8,9},{9,8},{10,11... | collective-permute-start | bytes 23592968 | tf_op jit(solution)/shard_map/cond/branch_0_fun/ppermute | solution.py:97
  175.5 5.4 %collective-permute-start.5 = (f32[8,128]{1,0:T(8,128)S(1)}, f32[8,128]{1,0:T(8,128)S(1)}, u32[]{:S(2)}, u32[]{:S(2)}) collective-permute-start(f32[8,128]{1,0:T(8,128)S(1)} %add_add_fusion.1), channel_id=1, source_target_pairs={{0,6},{1,7},{2,4},{3,5},{4,2},{5,3},{6,0},{7,1},{8,14},{9,15},{10,... | collective-permute-start | bytes 12296 | tf_op jit(solution)/shard_map/cond/branch_0_fun/ppermute | solution.py:92
  197.5 44.7 %all-to-all-start = ((bf16[4,320,640]{2,1,0:T(8,128)(2,1)}), bf16[4,320,640]{2,1,0:T(8,128)(2,1)}, u32[]{:S(2)}, u32[]{:S(2)}) async-start(bf16[4,320,640]{2,1,0:T(8,128)(2,1)} %get-tuple-element.123), calls=%async_computation | async-start | bytes 3276800 | tf_op jit(solution)/shard_map/cond/branch_0_fun/all_to_all | solution.py:439
  229.4 11.9 %collective-permute-start.13 = (f32[8,128]{1,0:T(8,128)S(1)}, f32[8,128]{1,0:T(8,128)S(1)}, u32[]{:S(2)}, u32[]{:S(2)}) collective-permute-start(f32[8,128]{1,0:T(8,128)S(1)} %add.279), channel_id=1, source_target_pairs={{0,4},{1,5},{2,6},{3,7},{4,0},{5,1},{6,2},{7,3},{8,12},{9,13},{10,... | collective-permute-start | bytes 12296 | tf_op jit(solution)/shard_map/cond/branch_0_fun/ppermute | solution.py:102
  (26 other events, 276.1 us)
